TPU v7x, 32 devices: a whole 2x2x4 slice. The times are simulated.
32 devices in a mesh: seq: 16 (over z, y, x), mp: 2 (over core).
Axes of the slice: x: 2, y: 2, z: 4, core: 2. Of those that a mesh axis runs over, the one named last changes fastest.
Arguments:
- tokens: bfloat16 [1024, 2, 1024], P('seq'), may hold values from -6 to 6
- segments: int32 [2, 1024], replicated, may hold values from 0 to 3, as said below
- routed: int32 [2, 128], replicated, may hold values from 0 to 1023, as said below
- router: bfloat16 [1024], replicated, may hold values from -0.0625 to 0.0625
- dense_attn_gain: bfloat16 [1024], replicated, may hold values from 0.5 to 1.5
- dense_qkv: bfloat16 [1024, 3, 1024], P(None, None, 'mp'), may hold values from -0.1875 to 0.1875
- dense_out: bfloat16 [1024, 1024], P('mp'), may hold values from -3 to 3
- dense_mlp_gain: bfloat16 [1024], replicated, may hold values from 0.5 to 1.5
- dense_up: bfloat16 [1024, 4096], P(None, 'mp'), may hold values from -0.1875 to 0.1875
- dense_down: bfloat16 [4096, 1024], P('mp'), may hold values from -0.09375 to 0.09375
- routed_attn_gain: bfloat16 [1024], replicated, may hold values from 0.5 to 1.5
- routed_qkv: bfloat16 [1024, 3, 1024], P(None, None, 'mp'), may hold values from -0.1875 to 0.1875
- routed_out: bfloat16 [1024, 1024], P('mp'), may hold values from -3 to 3
- routed_mlp_gain: bfloat16 [1024], replicated, may hold values from 0.5 to 1.5
- routed_up: bfloat16 [1024, 4096], P(None, 'mp'), may hold values from -0.1875 to 0.1875
- routed_down: bfloat16 [4096, 1024], P('mp'), may hold values from -0.09375 to 0.09375
- cotangent: bfloat16 [1024, 2, 1024], P('seq'), may hold values from -6 to 6
Outputs:
- output: float32 [1024, 2, 1024], P('seq')
- grad_tokens: float32 [1024, 2, 1024], P('seq')
- grad_dense_attn_gain: float32 [1024], P('seq')
- grad_dense_qkv: float32 [1024, 3, 1024], P('seq', None, 'mp')
- grad_dense_out: float32 [1024, 1024], P('mp', 'seq')
- grad_dense_mlp_gain: float32 [1024], P('seq')
- grad_dense_up: float32 [1024, 4096], P('seq', 'mp')
- grad_dense_down: float32 [4096, 1024], P('mp', 'seq')
- grad_routed_attn_gain: float32 [1024], P('seq')
- grad_routed_qkv: float32 [1024, 3, 1024], P('seq', None, 'mp')
- grad_routed_out: float32 [1024, 1024], P('mp', 'seq')
- grad_routed_mlp_gain: float32 [1024], P('seq')
- grad_routed_up: float32 [1024, 4096], P('seq', 'mp')
- grad_routed_down: float32 [4096, 1024], P('mp', 'seq')
- grad_router: float32 [1024], P('seq')
Inputs may be any that keep to these rules, and one draw needn't show every extreme that they name: `segments`: along each sequence the numbers start at 0 and never fall. One sequence of each draw, which one drawn from the seed, is a single document (all 0); every other holds exactly 4 documents. `routed`: each row lists 128 distinct positions of its sequence in increasing order. Of the 64 positions of a sequence on one index of seq at most 16 are listed, and exactly 16 on one index in every sequence.
All inputs are finite; a program needn't handle non-finite values.
Results may differ from a plain program's by a relative error of at most 0.024.
Values may be sent and summed in bfloat16 or wider, within the bound.
A program may use at most 192 MiB of HBM per device.

v0:
```python
import math

import jax
import jax.numpy as jnp
from jax import lax
from jax.sharding import PartitionSpec as P

HEAD_DIM = 64


EPSILON = 1e-06
NEGATIVE = -1e30
PRECISE = lax.Precision.HIGHEST


def rms_norm(hidden, gain):
    return hidden * lax.rsqrt(jnp.mean(hidden * hidden, axis=-1, keepdims=True) + EPSILON) * gain


def gelu_tanh(operand):
    return jax.nn.gelu(operand, approximate=True)


def model_sum(operand):
    return lax.psum(operand, "mp")


def block_loop(row_total, advance, carried):
    block_size = math.gcd(row_total, 512)
    return lax.fori_loop(
        0,
        row_total // block_size,
        lambda number, current: advance(current, number * block_size, block_size),
        carried,
    )


def key_mask(query_places, query_live, key_places, key_live, label_rows):
    query_labels = jnp.take_along_axis(label_rows, query_places, axis=0)
    key_labels = jnp.take_along_axis(label_rows, key_places, axis=0)
    allowed = jnp.transpose(key_places)[:, None, :] <= jnp.transpose(query_places)[:, :, None]
    allowed = allowed & (
        jnp.transpose(key_labels)[:, None, :] == jnp.transpose(query_labels)[:, :, None]
    )
    allowed = allowed & jnp.transpose(key_live)[:, None, :] & jnp.transpose(query_live)[:, :, None]
    return allowed[:, None]


def attend_forward(queries, key_rows, value_rows, own_places, own_live, row_info, label_rows):
    row_count, seq_count, head_count, head_size = queries.shape
    score_scale = head_size ** (-0.5)
    shape_rows = (seq_count, head_count, row_count)
    initial = (
        jnp.full(shape_rows, NEGATIVE, jnp.float32),
        jnp.zeros(shape_rows, jnp.float32),
        jnp.zeros(shape_rows + (head_size,), jnp.float32),
    )
    key_piece = lax.all_gather(key_rows, "seq", axis=0, tiled=True)
    value_piece = lax.all_gather(value_rows, "seq", axis=0, tiled=True)

    def advance(current, offset, block_size):
        highest, totals, summed = current
        key_block = lax.dynamic_slice_in_dim(key_piece, offset, block_size, 0).reshape(
            block_size, seq_count, head_count, head_size
        )
        value_block = lax.dynamic_slice_in_dim(value_piece, offset, block_size, 0).reshape(
            block_size, seq_count, head_count, head_size
        )
        key_places, key_live = row_info(offset, block_size)
        allowed = key_mask(own_places, own_live, key_places, key_live, label_rows)
        scores = (
            jnp.einsum("qshe,kshe->shqk", queries, key_block, preferred_element_type=jnp.float32)
            * score_scale
        )
        scores = jnp.where(allowed, scores, NEGATIVE)
        newest = jnp.maximum(highest, jnp.max(scores, axis=-1))
        weights = jnp.exp(scores - newest[..., None])
        factor = jnp.exp(highest - newest)
        totals = totals * factor + jnp.sum(weights, axis=-1)
        summed = summed * factor[..., None] + jnp.einsum(
            "shqk,kshe->shqe",
            weights.astype(jnp.bfloat16),
            value_block,
            preferred_element_type=jnp.float32,
        )
        return (newest, totals, summed)

    highest, totals, summed = block_loop(key_piece.shape[0], advance, initial)
    mixed_rows = jnp.transpose(summed / totals[..., None], (2, 0, 1, 3)).reshape(
        row_count, seq_count, head_count * head_size
    )
    return (mixed_rows, highest + jnp.log(totals), None)


def attend_backward(
    queries,
    key_rows,
    value_rows,
    grad_mixed,
    mixed_rows,
    log_sum,
    own_places,
    own_live,
    row_info,
    label_rows,
):
    row_count, seq_count, head_count, head_size = queries.shape
    score_scale = head_size ** (-0.5)
    grad_heads = grad_mixed.reshape(row_count, seq_count, head_count, head_size)
    offsets = jnp.sum(
        grad_heads.astype(jnp.float32)
        * mixed_rows.reshape(row_count, seq_count, head_count, head_size),
        axis=-1,
    )
    offsets_rows = jnp.transpose(offsets, (1, 2, 0))
    key_piece = lax.all_gather(key_rows, "seq", axis=0, tiled=True)
    value_piece = lax.all_gather(value_rows, "seq", axis=0, tiled=True)

    def advance(current, offset, block_size):
        key_block = lax.dynamic_slice_in_dim(key_piece, offset, block_size, 0).reshape(
            block_size, seq_count, head_count, head_size
        )
        value_block = lax.dynamic_slice_in_dim(value_piece, offset, block_size, 0).reshape(
            block_size, seq_count, head_count, head_size
        )
        key_places, key_live = row_info(offset, block_size)
        allowed = key_mask(own_places, own_live, key_places, key_live, label_rows)
        scores = (
            jnp.einsum("qshe,kshe->shqk", queries, key_block, preferred_element_type=jnp.float32)
            * score_scale
        )
        scores = jnp.where(allowed, scores, NEGATIVE)
        chances = jnp.exp(scores - log_sum[..., None])
        pushes = jnp.einsum(
            "qshe,kshe->shqk", grad_heads, value_block, preferred_element_type=jnp.float32
        )
        slopes = (chances * (pushes - offsets_rows[..., None])).astype(jnp.bfloat16)
        return current + jnp.einsum(
            "shqk,kshe->qshe", slopes, key_block, preferred_element_type=jnp.float32
        )

    grad_queries = block_loop(key_piece.shape[0], advance, jnp.zeros(queries.shape, jnp.float32))
    log_all, offsets_all = (
        lax.all_gather(jnp.transpose(log_sum, (2, 0, 1)), "seq", axis=0, tiled=True),
        lax.all_gather(offsets, "seq", axis=0, tiled=True),
    )
    own_keys = key_rows.reshape(row_count, seq_count, head_count, head_size)
    own_values = value_rows.reshape(row_count, seq_count, head_count, head_size)
    zero_rows = jnp.zeros(queries.shape, jnp.float32)
    query_flat = queries.reshape(row_count, seq_count, head_count * head_size)
    query_piece = lax.all_gather(query_flat, "seq", axis=0, tiled=True)
    grad_piece = lax.all_gather(grad_mixed, "seq", axis=0, tiled=True)

    def advance(current, offset, block_size):
        key_sum, value_sum = current
        query_block = lax.dynamic_slice_in_dim(query_piece, offset, block_size, 0).reshape(
            block_size, seq_count, head_count, head_size
        )
        grad_block = lax.dynamic_slice_in_dim(grad_piece, offset, block_size, 0).reshape(
            block_size, seq_count, head_count, head_size
        )
        block_log = jnp.transpose(
            lax.dynamic_slice_in_dim(log_all, offset, block_size, 0), (1, 2, 0)
        )
        block_offsets = jnp.transpose(
            lax.dynamic_slice_in_dim(offsets_all, offset, block_size, 0), (1, 2, 0)
        )
        query_places, query_live = row_info(offset, block_size)
        allowed = key_mask(query_places, query_live, own_places, own_live, label_rows)
        scores = (
            jnp.einsum("qshe,kshe->shqk", query_block, own_keys, preferred_element_type=jnp.float32)
            * score_scale
        )
        scores = jnp.where(allowed, scores, NEGATIVE)
        chances = jnp.exp(scores - block_log[..., None])
        pushes = jnp.einsum(
            "qshe,kshe->shqk", grad_block, own_values, preferred_element_type=jnp.float32
        )
        slopes = (chances * (pushes - block_offsets[..., None])).astype(jnp.bfloat16)
        key_sum = key_sum + jnp.einsum(
            "shqk,qshe->kshe", slopes, query_block, preferred_element_type=jnp.float32
        )
        value_sum = value_sum + jnp.einsum(
            "shqk,qshe->kshe",
            chances.astype(jnp.bfloat16),
            grad_block,
            preferred_element_type=jnp.float32,
        )
        return (key_sum, value_sum)

    key_sum, value_sum = block_loop(query_piece.shape[0], advance, (zero_rows, zero_rows))
    flat_shape = (row_count, seq_count, head_count * head_size)
    return (
        (grad_queries * score_scale).reshape(flat_shape),
        (key_sum * score_scale).reshape(flat_shape),
        value_sum.reshape(flat_shape),
    )


def block_forward(hidden, params, row_info, label_rows):
    attn_gain, qkv_weight, out_weight, mlp_gain, up_weight, down_weight = params
    row_count, seq_count, _ = hidden.shape
    head_width = qkv_weight.shape[2]
    head_count = head_width // HEAD_DIM
    own_places, own_live = row_info(lax.axis_index("seq") * row_count, row_count)
    normed = rms_norm(hidden, attn_gain.astype(jnp.float32)).astype(jnp.bfloat16)
    projected = jnp.einsum(
        "rsd,dce->rsce", normed, qkv_weight, preferred_element_type=jnp.float32
    ).astype(jnp.bfloat16)
    queries = projected[:, :, 0].reshape(row_count, seq_count, head_count, HEAD_DIM)
    key_rows = projected[:, :, 1]
    value_rows = projected[:, :, 2]
    mixed_rows, log_sum, kept_rows = attend_forward(
        queries, key_rows, value_rows, own_places, own_live, row_info, label_rows
    )
    mixed_low = mixed_rows.astype(jnp.bfloat16)
    attention = model_sum(
        jnp.einsum("rsh,hd->rsd", mixed_low, out_weight, preferred_element_type=jnp.float32)
    )
    middle = hidden + attention
    normed_mlp = rms_norm(middle, mlp_gain.astype(jnp.float32)).astype(jnp.bfloat16)
    before = jnp.einsum("rsd,df->rsf", normed_mlp, up_weight, preferred_element_type=jnp.float32)
    active = gelu_tanh(before).astype(jnp.bfloat16)
    feed_out = model_sum(
        jnp.einsum("rsf,fd->rsd", active, down_weight, preferred_element_type=jnp.float32)
    )
    stored = (
        hidden,
        normed,
        queries,
        key_rows,
        value_rows,
        mixed_rows,
        log_sum,
        mixed_low,
        middle,
        normed_mlp,
        before,
        active,
        own_places,
        own_live,
        kept_rows,
    )
    return (attention, middle, feed_out, stored)


def block_backward(incoming, stored, params, row_info, label_rows):
    attn_gain, qkv_weight, out_weight, mlp_gain, up_weight, down_weight = params
    (
        hidden,
        normed,
        queries,
        key_rows,
        value_rows,
        mixed_rows,
        log_sum,
        mixed_low,
        middle,
        normed_mlp,
        before,
        active,
        own_places,
        own_live,
        kept_rows,
    ) = stored
    incoming_low = incoming.astype(jnp.bfloat16)
    grad_down = jnp.einsum("rsf,rsd->fd", active, incoming_low, preferred_element_type=jnp.float32)
    grad_active = jnp.einsum(
        "rsd,fd->rsf", incoming_low, down_weight, preferred_element_type=jnp.float32
    )
    _, gelu_pull = jax.vjp(gelu_tanh, before)
    grad_before = gelu_pull(grad_active)[0].astype(jnp.bfloat16)
    grad_up = jnp.einsum("rsd,rsf->df", normed_mlp, grad_before, preferred_element_type=jnp.float32)
    grad_normed_mlp = model_sum(
        jnp.einsum("rsf,df->rsd", grad_before, up_weight, preferred_element_type=jnp.float32)
    )
    _, mlp_pull = jax.vjp(rms_norm, middle, mlp_gain.astype(jnp.float32))
    grad_middle, grad_mlp_gain = mlp_pull(grad_normed_mlp)
    along_low = (incoming + grad_middle).astype(jnp.bfloat16)
    grad_out = jnp.einsum("rsh,rsd->hd", mixed_low, along_low, preferred_element_type=jnp.float32)
    grad_mixed = jnp.einsum(
        "rsd,hd->rsh", along_low, out_weight, preferred_element_type=jnp.float32
    ).astype(jnp.bfloat16)
    grad_queries, grad_keys, grad_values = attend_backward(
        queries,
        key_rows,
        value_rows,
        grad_mixed,
        mixed_rows,
        log_sum,
        own_places,
        own_live,
        row_info,
        label_rows,
    )
    grad_projected = jnp.stack((grad_queries, grad_keys, grad_values), axis=2).astype(jnp.bfloat16)
    grad_qkv = jnp.einsum(
        "rsd,rsce->dce", normed, grad_projected, preferred_element_type=jnp.float32
    )
    grad_normed = model_sum(
        jnp.einsum("rsce,dce->rsd", grad_projected, qkv_weight, preferred_element_type=jnp.float32)
    )
    _, attn_pull = jax.vjp(rms_norm, hidden, attn_gain.astype(jnp.float32))
    grad_hidden, grad_attn_gain = attn_pull(grad_normed)
    return (
        grad_middle + grad_hidden,
        (grad_attn_gain, grad_qkv, grad_out, grad_mlp_gain, grad_up, grad_down),
    )


def on_device(
    tokens,
    segments,
    routed,
    router,
    dense_attn_gain,
    dense_qkv,
    dense_out,
    dense_mlp_gain,
    dense_up,
    dense_down,
    routed_attn_gain,
    routed_qkv,
    routed_out,
    routed_mlp_gain,
    routed_up,
    routed_down,
    cotangent,
):
    group_rows, seq_count, _ = tokens.shape
    devices = lax.axis_size("seq")
    my_index = lax.axis_index("seq")
    capacity = routed.shape[1]
    most_rows = group_rows // 4
    label_rows = jnp.transpose(segments)
    route_rows = jnp.transpose(routed)
    local_ids = jnp.arange(group_rows, dtype=jnp.int32)
    bounds = jnp.arange(devices + 1, dtype=jnp.int32) * group_rows
    starts = jnp.sum((routed[None, :, :] < bounds[:, None, None]).astype(jnp.int32), axis=2)
    first_rank = starts[my_index]
    routed_here = starts[my_index + 1] - first_rank
    dense_params = (dense_attn_gain, dense_qkv, dense_out, dense_mlp_gain, dense_up, dense_down)
    routed_params = (
        routed_attn_gain,
        routed_qkv,
        routed_out,
        routed_mlp_gain,
        routed_up,
        routed_down,
    )

    def dense_info(first_row, row_total):
        places = first_row + jnp.broadcast_to(
            jnp.arange(row_total, dtype=jnp.int32)[:, None], (row_total, seq_count)
        )
        return (places, jnp.ones((row_total, seq_count), jnp.bool_))

    slot_rows = jnp.arange(most_rows, dtype=jnp.int32)
    is_live = slot_rows[:, None] < routed_here[None, :]
    hold_places = (
        jnp.take_along_axis(
            route_rows, jnp.clip(first_rank[None, :] + slot_rows[:, None], 0, capacity - 1), axis=0
        )
        - my_index * group_rows
    )
    hold_table = (
        (jnp.transpose(hold_places)[:, :, None] == local_ids[None, None, :])
        & jnp.transpose(is_live)[:, :, None]
    ).astype(jnp.bfloat16)

    def select_rows(rows_in):
        return jnp.einsum(
            "smc,csd->msd", hold_table, rows_in, preferred_element_type=jnp.float32
        ).astype(jnp.bfloat16)

    def restore_rows(rows_in):
        return jnp.einsum("smc,msd->csd", hold_table, rows_in, preferred_element_type=jnp.float32)

    def routed_info(first_row, row_total):
        number = first_row + jnp.arange(row_total, dtype=jnp.int32)
        source = number // most_rows
        within = number % most_rows
        base = jnp.take(starts, source, axis=0)
        filled = jnp.take(starts, source + 1, axis=0) - base
        rank_rows = jnp.clip(base + within[:, None], 0, capacity - 1)
        return (jnp.take_along_axis(route_rows, rank_rows, axis=0), within[:, None] < filled)

    hidden = tokens.astype(jnp.float32)
    _, middle, feed_out, dense_stored = block_forward(hidden, dense_params, dense_info, label_rows)
    first_out = middle + feed_out
    lifted = select_rows(first_out.astype(jnp.bfloat16))
    routed_attention, _, routed_feed, routed_stored = block_forward(
        lifted.astype(jnp.float32), routed_params, routed_info, label_rows
    )
    sent_rows = (routed_attention + routed_feed).astype(jnp.bfloat16)
    returned = restore_rows(sent_rows)
    router_float = router.astype(jnp.float32)
    gate_value = jax.nn.sigmoid(jnp.einsum("csd,d->cs", first_out, router_float, precision=PRECISE))
    output = first_out + gate_value[:, :, None] * returned
    grad_output = cotangent.astype(jnp.float32)
    grad_sent = select_rows((gate_value[:, :, None] * grad_output).astype(jnp.bfloat16))
    grad_logit = jnp.sum(grad_output * returned, axis=-1) * gate_value * (1.0 - gate_value)
    grad_router = jnp.einsum("cs,csd->d", grad_logit, first_out, precision=PRECISE)
    grad_first = grad_output + grad_logit[:, :, None] * router_float
    routed_branch, routed_grads = block_backward(
        grad_sent.astype(jnp.float32), routed_stored, routed_params, routed_info, label_rows
    )
    grad_first = grad_first + restore_rows(routed_branch.astype(jnp.bfloat16))
    dense_branch, dense_grads = block_backward(
        grad_first, dense_stored, dense_params, dense_info, label_rows
    )
    grad_tokens = grad_first + dense_branch
    summed_all = (
        lax.psum_scatter(dense_grads[0], "seq", scatter_dimension=0, tiled=True),
        lax.psum_scatter(dense_grads[1], "seq", scatter_dimension=0, tiled=True),
        lax.psum_scatter(dense_grads[2], "seq", scatter_dimension=1, tiled=True),
        lax.psum_scatter(dense_grads[3], "seq", scatter_dimension=0, tiled=True),
        lax.psum_scatter(dense_grads[4], "seq", scatter_dimension=0, tiled=True),
        lax.psum_scatter(dense_grads[5], "seq", scatter_dimension=1, tiled=True),
        lax.psum_scatter(routed_grads[0], "seq", scatter_dimension=0, tiled=True),
        lax.psum_scatter(routed_grads[1], "seq", scatter_dimension=0, tiled=True),
        lax.psum_scatter(routed_grads[2], "seq", scatter_dimension=1, tiled=True),
        lax.psum_scatter(routed_grads[3], "seq", scatter_dimension=0, tiled=True),
        lax.psum_scatter(routed_grads[4], "seq", scatter_dimension=0, tiled=True),
        lax.psum_scatter(routed_grads[5], "seq", scatter_dimension=1, tiled=True),
        lax.psum_scatter(grad_router, "seq", scatter_dimension=0, tiled=True),
    )
    dense_sums = tuple(summed_all[0:6])
    routed_sums = tuple(summed_all[6:13])
    return (output, grad_tokens) + tuple(dense_sums) + tuple(routed_sums)


def solution(mesh):
    in_specs = (
        P("seq", None, None),
        P(),
        P(),
        P(),
        P(),
        P(None, None, "mp"),
        P("mp", None),
        P(),
        P(None, "mp"),
        P("mp", None),
        P(),
        P(None, None, "mp"),
        P("mp", None),
        P(),
        P(None, "mp"),
        P("mp", None),
        P("seq", None, None),
    )
    out_specs = (
        P("seq", None, None),
        P("seq", None, None),
        P("seq"),
        P("seq", None, "mp"),
        P("mp", "seq"),
        P("seq"),
        P("seq", "mp"),
        P("mp", "seq"),
        P("seq"),
        P("seq", None, "mp"),
        P("mp", "seq"),
        P("seq"),
        P("seq", "mp"),
        P("mp", "seq"),
        P("seq"),
    )
    return jax.shard_map(
        on_device, mesh=mesh, in_specs=in_specs, out_specs=out_specs, check_vma=False
    )
```

profile of v0, /device:TPU:0, one launch (start us, length us, event | category | flops | bytes accessed | tf_op | source)
XLA Modules:
  0.0 2057.3 jit_solution(5896729013450336018)
XLA Ops:
  46.7 29.0 %all-gather.13.cloned.1.call-done = bf16[1024,2,1,512]{3,0,2,1:T(8,128)(2,1)} async-done(((bf16[64,2,1,512]{3,0,2,1:T(8,128)(2,1)}), bf16[1024,2,1,512]{3,0,2,1:T(8,128)(2,1)}) %all-gather.13.cloned.1.call-update) | async-done | bytes 2097168 | tf_op jit(solution)/shard_map/all_gather | solution.py:58
  79.7 58.6 %all-gather.15.cloned.1.call-done = bf16[1024,2,1,512]{3,0,2,1:T(8,128)(2,1)} async-done(((bf16[64,2,1,512]{3,0,2,1:T(8,128)(2,1)}), bf16[1024,2,1,512]{3,0,2,1:T(8,128)(2,1)}) %all-gather.15.cloned.1.call-update) | async-done | bytes 2097168 | tf_op jit(solution)/shard_map/all_gather | solution.py:59
  142.2 50.8 %while.33 = (s32[]{:T(128)}, f32[2,8,64]{2,1,0:T(8,128)S(1)}, f32[2,8,64]{2,1,0:T(8,128)S(1)}, f32[2,8,64,64]{3,2,1,0:T(8,128)}, s32[1024,2]{0,1:T(2,128)S(1)}, ...) while((s32[]{:T(128)}, f32[2,8,64]{2,1,0:T(8,128)S(1)}, ...), condition=%wide.region_4.7_spmd.clone, body=%wide.region_1.6_spmd.clone.sunk | while | flops 138299392 | bytes 21897700 | solution.py:30
  144.3 9.1 gather_fusion
  169.7 9.1 gather_fusion
  203.7 13.2 all-reduce.15.cloned.1.call-done
  229.2 15.6 all-reduce.17.cloned.1.call-done
  251.1 46.0 %all-gather.4 = bf16[256,2,1,512]{3,0,2,1:T(8,128)(2,1)} all-gather(bf16[16,2,1,512]{3,0,2,1:T(8,128)(2,1)S(1)} %get-tuple-element.1320), channel_id=6, replica_groups=mesh['seq'=16,'mp'=2] {'seq'}, dimensions={0}, use_global_device_ids=true | all-gather | bytes 557056 | tf_op jit(solution)/shard_map/all_gather | solution.py:151
  297.1 40.7 %all-gather.2 = bf16[256,2,1,512]{3,0,2,1:T(8,128)(2,1)} all-gather(bf16[16,2,1,512]{3,0,2,1:T(8,128)(2,1)S(1)} %get-tuple-element.1322), channel_id=4, replica_groups=mesh['seq'=16,'mp'=2] {'seq'}, dimensions={0}, use_global_device_ids=true | all-gather | bytes 557056 | tf_op jit(solution)/shard_map/all_gather | solution.py:58
  338.6 42.8 %all-gather.3 = bf16[256,2,1,512]{3,0,2,1:T(8,128)(2,1)} all-gather(bf16[16,2,1,512]{3,0,2,1:T(8,128)(2,1)S(1)} %get-tuple-element.1321), channel_id=5, replica_groups=mesh['seq'=16,'mp'=2] {'seq'}, dimensions={0}, use_global_device_ids=true | all-gather | bytes 557056 | tf_op jit(solution)/shard_map/all_gather | solution.py:59
  397.9 39.2 %all_gather.45 = f32[256,2,8]{2,1,0:T(2,128)} all-gather(f32[16,2,8]{2,1,0:T(2,128)S(1)} %copy.410), channel_id=1, replica_groups=mesh['seq'=16,'mp'=2] {'seq'}, dimensions={0}, use_global_device_ids=true | all-gather | bytes 17408 | tf_op jit(solution)/shard_map/all_gather | solution.py:144
  457.2 12.1 all-reduce.21.cloned.1.call-done
  474.4 46.0 %all_gather.46 = bf16[256,2,512]{2,0,1:T(8,128)(2,1)} all-gather(bf16[16,2,512]{2,0,1:T(8,128)(2,1)S(1)} %convolution_convert_fusion.4), channel_id=1, replica_groups=mesh['seq'=16,'mp'=2] {'seq'}, dimensions={0}, use_global_device_ids=true | all-gather | bytes 557056 | tf_op jit(solution)/shard_map/all_gather | solution.py:152
  526.9 39.6 %all_gather.47 = f32[256,2,8]{2,1,0:T(2,128)} all-gather(f32[16,2,8]{2,1,0:T(2,128)} %copy.414), channel_id=1, replica_groups=mesh['seq'=16,'mp'=2] {'seq'}, dimensions={0}, use_global_device_ids=true | all-gather | bytes 17408 | tf_op jit(solution)/shard_map/all_gather | solution.py:145
  582.4 15.1 all-reduce.27.cloned.1.call-done
  621.8 51.3 %all_gather.49 = f32[1024,2,8]{2,1,0:T(2,128)} all-gather(f32[64,2,8]{2,1,0:T(2,128)S(1)} %bitcast.477), channel_id=1, replica_groups=mesh['seq'=16,'mp'=2] {'seq'}, dimensions={0}, use_global_device_ids=true | all-gather | bytes 69632 | tf_op jit(solution)/shard_map/all_gather | solution.py:144
  686.4 52.5 %while.34 = (s32[]{:T(128)}, f32[64,2,8,64]{0,3,2,1:T(8,128)}, bf16[1024,2,512]{0,2,1:T(8,128)(2,1)}, s32[1024,2]{0,1:T(2,128)S(1)}, s32[64,2]{0,1:T(2,128)}, /*...) while((s32[]{:T(128)}, f32[64,2,8,64]{0,3,2,1:T(8,128)}, ...), condition=%wide.region_25.34_spmd.clone, body=%wide.region_24.33_spmd.clone.sunk | while | flops 204813312 | bytes 16761381 | solution.py:30
  689.1 9.1 gather_fusion.1
  715.3 9.1 gather_fusion.1
  740.8 49.1 %all_gather.51 = f32[1024,2,8]{2,1,0:T(2,128)} all-gather(f32[64,2,8]{2,1,0:T(2,128)} %copy.430), channel_id=1, replica_groups=mesh['seq'=16,'mp'=2] {'seq'}, dimensions={0}, use_global_device_ids=true | all-gather | bytes 69632 | tf_op jit(solution)/shard_map/all_gather | solution.py:145
  791.9 62.3 %while.35 = (s32[]{:T(128)}, f32[64,2,8,64]{0,3,2,1:T(8,128)}, f32[64,2,8,64]{0,3,2,1:T(8,128)}, bf16[1024,2,512]{2,0,1:T(8,128)(2,1)}, s32[64,2]{0,1:T(2,128)},...) while((s32[]{:T(128)}, f32[64,2,8,64]{0,3,2,1:T(8,128)}, ...), condition=%wide.region_27.36_spmd.clone, body=%wide.region_26.35_spmd.clone.sunk | while | flops 272577536 | bytes 21635604 | solution.py:30
  792.3 9.1 gather_fusion.2
  823.4 9.1 gather_fusion.2
  888.0 6.0 convolution_bitcast_fusion.3
  906.6 72.1 %all-reduce.5 = (f32[1024]{0:T(1024)S(1)}, f32[1024]{0:T(1024)S(1)}, f32[1024]{0:T(1024)S(1)}, f32[1024]{0:T(1024)S(1)}, f32[1024]{0:T(1024)S(1)}) all-reduce(f32[1024]{0:T(1024)S(1)} %get-tuple-element.1210, f32[1024]{0:T(1024)S(1)} %copy-done.70, f32[1024]{0:T(1024)S(1)} %copy-done.69, ...), channel_id=8, replica_groups=mesh['seq'=16,'mp'=2] {'seq'}, use_global_device_ids=true, to_apply=%region_31.40.clone | all-reduce | flops 5120 | bytes 40960
  984.6 57.0 %reduce-scatter.11.cloned.1.call-done = f32[512,64]{0,1:T(8,128)} async-done(((f32[512,1024]{0,1:T(8,128)}), f32[512,64]{0,1:T(8,128)}) %reduce-scatter.11.cloned.1.call-update) | async-done | bytes 131088 | tf_op jit(solution)/shard_map/reduce_scatter | solution.py:416
  1041.6 135.9 %reduce-scatter.17.cloned.1.call-done = f32[64,3,512]{2,0,1:T(8,128)} async-done(((f32[1024,3,512]{2,0,1:T(8,128)}), f32[64,3,512]{2,0,1:T(8,128)}) %reduce-scatter.17.cloned.1.call-update) | async-done | bytes 393232 | tf_op jit(solution)/shard_map/reduce_scatter | solution.py:421
  1177.6 182.0 %reduce-scatter.21.cloned.1.call-done = f32[64,2048]{1,0:T(8,128)} async-done(((f32[1024,2048]{1,0:T(8,128)}), f32[64,2048]{1,0:T(8,128)}) %reduce-scatter.21.cloned.1.call-update) | async-done | bytes 524304 | tf_op jit(solution)/shard_map/reduce_scatter | solution.py:424
  1359.6 183.1 %reduce-scatter.23.cloned.1.call-done = f32[2048,64]{0,1:T(8,128)} async-done(((f32[2048,1024]{0,1:T(8,128)}), f32[2048,64]{0,1:T(8,128)}) %reduce-scatter.23.cloned.1.call-update) | async-done | bytes 524304 | tf_op jit(solution)/shard_map/reduce_scatter | solution.py:425
  1542.7 183.1 %reduce-scatter.13.cloned.1.call-done = f32[64,2048]{1,0:T(8,128)} async-done(((f32[1024,2048]{1,0:T(8,128)}), f32[64,2048]{1,0:T(8,128)}) %reduce-scatter.13.cloned.1.call-update) | async-done | bytes 524304 | tf_op jit(solution)/shard_map/reduce_scatter | solution.py:418
  1725.8 183.1 %reduce-scatter.15.cloned.1.call-done = f32[2048,64]{0,1:T(8,128)} async-done(((f32[2048,1024]{0,1:T(8,128)}), f32[2048,64]{0,1:T(8,128)}) %reduce-scatter.15.cloned.1.call-update) | async-done | bytes 524304 | tf_op jit(solution)/shard_map/reduce_scatter | solution.py:419
  1908.9 141.6 %reduce-scatter.9.cloned.1.call-done = f32[64,3,512]{2,0,1:T(8,128)} async-done(((f32[1024,3,512]{2,0,1:T(8,128)}), f32[64,3,512]{2,0,1:T(8,128)}) %reduce-scatter.9.cloned.1.call-update) | async-done | bytes 393232 | tf_op jit(solution)/shard_map/reduce_scatter | solution.py:415
  (543 shorter events, 344.2 us)
Async XLA Ops:
  7.2 68.5 %all-gather.13.cloned.1.call-start = ((), (), s32[]{:S(2)}) async-start(), calls=%async_computation.23 | async-start | bytes 2228224 | tf_op jit(solution)/shard_map/all_gather | solution.py:58
  12.1 126.1 %all-gather.15.cloned.1.call-start = ((), (), s32[]{:S(2)}) async-start(), calls=%async_computation.24 | async-start | bytes 2228224 | tf_op jit(solution)/shard_map/all_gather | solution.py:59
  12.9 204.1 %all-reduce.15.cloned.1.call-start = ((), (), s32[]{:S(2)}) async-start(), calls=%async_computation.8 | async-start | bytes 1048576 | tf_op jit(solution)/shard_map/psum | solution.py:25
  199.5 45.3 %all-reduce.17.cloned.1.call-start = ((), (), s32[]{:S(2)}) async-start(), calls=%async_computation.9 | async-start | bytes 1048576 | tf_op jit(solution)/shard_map/psum | solution.py:25
  224.8 219.2 %all-reduce.19.cloned.1.call-start = ((), (), s32[]{:S(2)}) async-start(), calls=%async_computation.10 | async-start | bytes 262144 | tf_op jit(solution)/shard_map/psum | solution.py:25
  225.1 377.3 %copy-start.51 = (f32[1024]{0:T(1024)}, f32[1024]{0:T(1024)S(1)}, u32[]{:S(2)}) copy-start(f32[1024]{0:T(1024)S(1)} %convert_element_type.188) | copy-start | bytes 12292
  227.2 375.2 %copy-start.38 = (f32[1024]{0:T(1024)}, f32[1024]{0:T(1024)S(1)}, u32[]{:S(2)}) copy-start(f32[1024]{0:T(1024)S(1)} %convert_element_type.194) | copy-start | bytes 12292
  247.2 50.0 %copy-start.84 = (f32[16,2]{0,1:T(2,128)}, f32[16,2]{0,1:T(2,128)S(1)}, u32[]{:S(2)}) copy-start(f32[16,2]{0,1:T(2,128)S(1)} %get-tuple-element.1328) | copy-start | bytes 388
  247.2 50.0 %copy-start.63 = (f32[16,2]{0,1:T(2,128)}, f32[16,2]{0,1:T(2,128)S(1)}, u32[]{:S(2)}) copy-start(f32[16,2]{0,1:T(2,128)S(1)} %fusion.200) | copy-start | bytes 388
  391.1 50.2 %copy-start.60 = (pred[2,256,16]{1,2,0:T(8,128)(4,1)S(1)}, pred[2,256,16]{1,2,0:T(8,128)(4,1)}, u32[]{:S(2)}) copy-start(pred[2,256,16]{1,2,0:T(8,128)(4,1)} %and_and_fusion) | copy-start | bytes 24580
  395.0 74.3 %all-reduce.21.cloned.1.call-start = ((), (), s32[]{:S(2)}) async-start(), calls=%async_computation.11 | async-start | bytes 262144 | tf_op jit(solution)/shard_map/psum | solution.py:25
  445.0 157.4 %copy-start.53 = (f32[16,2]{0,1:T(2,128)}, f32[16,2]{0,1:T(2,128)S(1)}, u32[]{:S(2)}) copy-start(f32[16,2]{0,1:T(2,128)S(1)} %fusion.201) | copy-start | bytes 388
  453.4 144.0 %all-reduce.27.cloned.1.call-start = ((), (), s32[]{:S(2)}) async-start(), calls=%async_computation.26 | async-start | bytes 524288 | tf_op jit(solution)/shard_map/psum | solution.py:25
  471.0 49.5 %copy-start.80 = (f32[16,2]{0,1:T(2,128)}, f32[16,2]{0,1:T(2,128)S(1)}, u32[]{:S(2)}) copy-start(f32[16,2]{0,1:T(2,128)S(1)} %multiply_multiply_fusion.7) | copy-start | bytes 388
  524.4 47.7 %copy-start.44 = (bf16[16,2,8,64]{3,2,0,1:T(8,128)(2,1)S(1)}, bf16[16,2,8,64]{3,2,0,1:T(8,128)(2,1)}, u32[]{:S(2)}) copy-start(bf16[16,2,8,64]{3,2,0,1:T(8,128)(2,1)} %reshape_squeeze.21) | copy-start | bytes 98308
  526.9 50.7 %copy-start.45 = (bf16[16,2,1,512]{3,0,1,2:T(8,128)(2,1)}, bf16[16,2,1,512]{3,0,1,2:T(8,128)(2,1)S(1)}, u32[]{:S(2)}) copy-start(bf16[16,2,1,512]{3,0,1,2:T(8,128)(2,1)S(1)} %stack_reshape.24) | copy-start | bytes 98308
  581.2 93.9 %all-reduce.23.cloned.1.call-start = ((), (), s32[]{:S(2)}) async-start(), calls=%async_computation.12 | async-start | bytes 1048576 | tf_op jit(solution)/shard_map/psum | solution.py:25
  611.5 180.3 %all-gather.17.cloned.1.call-start = ((), (), s32[]{:S(2)}) async-start(), calls=%async_computation.25 | async-start | bytes 2228224 | tf_op jit(solution)/shard_map/all_gather | solution.py:151
  612.3 179.6 %all-gather.11.cloned.1.call-start = ((), (), s32[]{:S(2)}) async-start(), calls=%async_computation.13 | async-start | bytes 2228224 | tf_op jit(solution)/shard_map/all_gather | solution.py:152
  614.1 61.0 %copy-start.56 = (f32[64,2]{0,1:T(2,128)S(1)}, f32[64,2]{0,1:T(2,128)}, u32[]{:S(2)}) copy-start(f32[64,2]{0,1:T(2,128)} %copy-done.55) | copy-start | bytes 1540
  617.7 59.5 %copy-start.89 = (f32[64,2]{0,1:T(2,128)S(1)}, f32[64,2]{0,1:T(2,128)}, u32[]{:S(2)}) copy-start(f32[64,2]{0,1:T(2,128)} %copy-done.88) | copy-start | bytes 1540
  682.4 222.9 %all-reduce.25.cloned.1.call-start = ((), (), s32[]{:S(2)}) async-start(), calls=%async_computation.14 | async-start | bytes 1048576 | tf_op jit(solution)/shard_map/psum | solution.py:25
  861.0 123.7 %reduce-scatter.19.cloned.1.call-start = ((), (), s32[]{:S(2)}) async-start(), calls=%async_computation.20 | async-start | bytes 2228224 | tf_op jit(solution)/shard_map/reduce_scatter | solution.py:422
  862.9 178.7 %reduce-scatter.11.cloned.1.call-start = ((), (), s32[]{:S(2)}) async-start(), calls=%async_computation.16 | async-start | bytes 2228224 | tf_op jit(solution)/shard_map/reduce_scatter | solution.py:416
  865.7 311.9 %reduce-scatter.17.cloned.1.call-start = ((), (), s32[]{:S(2)}) async-start(), calls=%async_computation.19 | async-start | bytes 6684672 | tf_op jit(solution)/shard_map/reduce_scatter | solution.py:421
  870.2 489.4 %reduce-scatter.21.cloned.1.call-start = ((), (), s32[]{:S(2)}) async-start(), calls=%async_computation.21 | async-start | bytes 8912896 | tf_op jit(solution)/shard_map/reduce_scatter | solution.py:424
  875.8 666.9 %reduce-scatter.23.cloned.1.call-start = ((), (), s32[]{:S(2)}) async-start(), calls=%async_computation.22 | async-start | bytes 8912896 | tf_op jit(solution)/shard_map/reduce_scatter | solution.py:425
  881.4 844.4 %reduce-scatter.13.cloned.1.call-start = ((), (), s32[]{:S(2)}) async-start(), calls=%async_computation.17 | async-start | bytes 8912896 | tf_op jit(solution)/shard_map/reduce_scatter | solution.py:418
  888.0 1020.9 %reduce-scatter.15.cloned.1.call-start = ((), (), s32[]{:S(2)}) async-start(), calls=%async_computation.18 | async-start | bytes 8912896 | tf_op jit(solution)/shard_map/reduce_scatter | solution.py:419
  894.0 1156.5 %reduce-scatter.9.cloned.1.call-start = ((), (), s32[]{:S(2)}) async-start(), calls=%async_computation.15 | async-start | bytes 6684672 | tf_op jit(solution)/shard_map/reduce_scatter | solution.py:415
  899.8 81.8 %copy-start.83 = (f32[64,2]{0,1:T(2,128)S(1)}, f32[64,2]{0,1:T(2,128)}, u32[]{:S(2)}) copy-start(f32[64,2]{0,1:T(2,128)} %copy-done.82) | copy-start | bytes 1540
  899.8 81.8 %copy-start.79 = (f32[64,2]{0,1:T(2,128)S(1)}, f32[64,2]{0,1:T(2,128)}, u32[]{:S(2)}) copy-start(f32[64,2]{0,1:T(2,128)} %copy-done.78) | copy-start | bytes 1540
  (97 other events, 540.8 us)
Sparse Core Ops, SparseCore 0:
  12.3 63.3 all-gather.12
  79.0 59.2 all-gather.14
  199.6 17.2 all-reduce.14
  224.9 19.8 all-reduce.16
  395.1 13.7 all-reduce.18
  453.6 15.6 all-reduce.20
  581.4 16.0 all-reduce.26
  611.6 19.8 all-reduce.22
  634.3 63.1 all-gather.16
  700.7 63.8 all-gather.10
  861.1 14.5 all-reduce.24
  878.5 81.6 reduce-scatter.18
  963.1 78.4 reduce-scatter.10
  1044.5 133.0 reduce-scatter.16
  1180.4 179.1 reduce-scatter.20
  1362.4 180.2 reduce-scatter.22
  1545.5 180.2 reduce-scatter.12
  1728.6 180.2 reduce-scatter.14
  1911.9 138.6 reduce-scatter.8
where the time goes:
time: 2070 us; the launch traced here: 2060 us
  waiting for transfers between devices  1210 us (58%)
  blocking collectives  427 us (21%)
  local copies, waits for them, and re-layouts  200 us (10%)
  matrix products  135 us (7%)
  other arithmetic  66.1 us (3%)
    reduce_scatter x1, waiting for transfers between devices, on_device(): lax.psum_scatter(routed_grads[5], 'seq', scatter_dimension=1, tiled=True)  183 us
    reduce_scatter x1, waiting for transfers between devices, on_device(): lax.psum_scatter(dense_grads[4], 'seq', scatter_dimension=0, tiled=True)  183 us
    reduce_scatter x1, waiting for transfers between devices, on_device(): lax.psum_scatter(dense_grads[5], 'seq', scatter_dimension=1, tiled=True)  183 us
    reduce_scatter x1, waiting for transfers between devices, on_device(): lax.psum_scatter(routed_grads[4], 'seq', scatter_dimension=0, tiled=True)  182 us
    reduce_scatter x1, waiting for transfers between devices, on_device(): lax.psum_scatter(dense_grads[1], 'seq', scatter_dimension=0, tiled=True)  142 us
    reduce_scatter x1, waiting for transfers between devices, on_device(): lax.psum_scatter(routed_grads[1], 'seq', scatter_dimension=0, tiled=True)  136 us
    all_gather x2, blocking collectives, attend_backward(): lax.all_gather(jnp.transpose(log_sum, (2, 0, 1)), 'seq', axis=0, tiled=True)  90.5 us
    all_gather x2, blocking collectives, attend_backward(): lax.all_gather(offsets, 'seq', axis=0, tiled=True)  88.7 us
  transfers between devices with their start and end apart: 19, of which 13 were waited for; matrix products, arithmetic and copies ran while one was open for 9% of the time, Pallas kernels for 0%

commit v1 on v0

--- a/solution.py
+++ b/solution.py
@@ -1,8 +1,11 @@
 import math
+import types
 
 import jax
 import jax.numpy as jnp
 from jax import lax
+from jax.experimental import pallas as pl
+from jax.experimental.pallas import tpu as pltpu
 from jax.sharding import PartitionSpec as P
 
 HEAD_DIM = 64
@@ -430,6 +433,874 @@
     return (output, grad_tokens) + tuple(dense_sums) + tuple(routed_sums)
 
 
+BF = jnp.bfloat16
+LIMIT = 63 * 1024 * 1024
+F32 = jnp.float32
+MESH = pl.DeviceIdType.MESH
+COLS = ((0, 1536), (1536, 512), (2048, 2048), (4096, 2048))
+
+
+def dot(a, b):
+    return lax.dot_general(a, b, (((1,), (0,)), ((), ())), preferred_element_type=F32)
+
+
+def dot_t(a, b):
+    return lax.dot_general(a, b, (((1,), (1,)), ((), ())), preferred_element_type=F32)
+
+
+def dot_l(a, b):
+    return lax.dot_general(a, b, (((0,), (0,)), ((), ())), preferred_element_type=F32)
+
+
+def swap_halves(tile):
+    return pltpu.roll(tile, 64, 1)
+
+
+def low_lanes(rows):
+    return lax.broadcasted_iota(jnp.int32, (rows, 128), 1) < 64
+
+
+def inverse_rms(rows):
+    return lax.rsqrt(jnp.mean(rows * rows, axis=1, keepdims=True) + EPSILON)
+
+
+def norm_back(grad, rows, gain):
+    inverse = inverse_rms(rows)
+    unit = rows * inverse
+    pulled = grad * gain
+    grad_rows = inverse * (pulled - unit * jnp.mean(pulled * unit, axis=1, keepdims=True))
+    return grad_rows, jnp.sum(grad * unit, axis=0, keepdims=True)
+
+
+class Env:
+    def __init__(self, refs, sems, seq_size):
+        self.b = refs
+        self.sems = sems
+        self.count = 0
+        self.sends = []
+        self.flying = {}
+        self.stores = {}
+        self.stored = 0
+        self.barrier_done = False
+        self.n = seq_size
+        self.s = lax.axis_index("seq")
+        self.c = lax.axis_index("mp")
+        self.q = lax.rem(self.s, 4)
+        self.z = lax.div(self.s, 4)
+
+    def sem(self):
+        self.count += 1
+        return self.sems.at[self.count - 1]
+
+    def greet(self):
+        barrier = pltpu.get_barrier_semaphore()
+
+        def signal(step, _):
+            other = lax.rem(self.s + step, self.n)
+            pl.semaphore_signal(barrier, inc=1, device_id=(other, self.c), device_id_type=MESH)
+            return 0
+
+        lax.fori_loop(1, self.n, signal, 0)
+        pl.semaphore_signal(barrier, inc=1, device_id=(self.s, 1 - self.c), device_id_type=MESH)
+
+    def meet(self):
+        if not self.barrier_done:
+            pl.semaphore_wait(pltpu.get_barrier_semaphore(), self.n)
+            self.barrier_done = True
+
+    def remote(self, src, dst, send, recv, seq, core):
+        return pltpu.make_async_remote_copy(
+            src_ref=src,
+            dst_ref=dst,
+            send_sem=send,
+            recv_sem=recv,
+            device_id=(seq, core),
+            device_id_type=MESH,
+        )
+
+    def exchange(self, send_ref, recv_ref):
+        self.meet()
+        send, recv = self.sem(), self.sem()
+        n = self.n
+
+        def start(step, _):
+            other = lax.rem(self.s + step, n)
+            self.remote(
+                send_ref.at[other], recv_ref.at[self.s], send, recv, other, self.c
+            ).start()
+            return 0
+
+        lax.fori_loop(1, n, start, 0)
+        recv_ref[pl.ds(self.s, 1)] = send_ref[pl.ds(self.s, 1)]
+        whole = self.remote(
+            send_ref.at[pl.ds(0, n - 1)],
+            recv_ref.at[pl.ds(0, n - 1)],
+            send,
+            recv,
+            lax.rem(self.s + 1, n),
+            self.c,
+        )
+        self.sends.append(whole)
+        return whole.wait_recv
+
+    def core_sum(self, layer, half, chunk, sink):
+        self.meet()
+        send_ref, recv_ref = layer.b.ps.at[half], layer.b.pr.at[half]
+        copies = []
+        for number in range(4):
+            earlier = self.flying.pop((layer.packed, half, number), None)
+            if earlier is not None:
+                earlier.wait_send()
+            send_ref[number] = chunk(number).astype(BF)
+            copy = self.remote(
+                send_ref.at[number], recv_ref.at[number], self.sem(), self.sem(), self.s, 1 - self.c
+            )
+            copy.start()
+            copies.append(copy)
+            self.flying[(layer.packed, half, number)] = copy
+        for number, copy in enumerate(copies):
+            copy.wait_recv()
+            sink(number, send_ref[number].astype(F32) + recv_ref[number].astype(F32))
+
+    def plane_send(self, pieces, recv_piece, wait_piece):
+        self.meet()
+        send, recv = self.sem(), self.sem()
+        for step in range(1, 4):
+            other = lax.rem(self.q + step, 4)
+            self.remote(
+                pieces(other), recv_piece, send, recv, self.z * 4 + other, self.c
+            ).start()
+        whole = self.remote(wait_piece, wait_piece, send, recv, self.z * 4 + lax.rem(self.q + 1, 4), self.c)
+        self.sends.append(whole)
+        return whole.wait_recv
+
+    def line_send(self, pieces, recv_piece, wait_piece):
+        self.meet()
+        send, recv = self.sem(), self.sem()
+        for step in range(1, 4):
+            other = lax.rem(self.z + step, 4)
+            self.remote(
+                pieces(other), recv_piece(step), send, recv, other * 4 + self.q, self.c
+            ).start()
+        whole = self.remote(wait_piece, wait_piece, send, recv, lax.rem(self.z + 1, 4) * 4 + self.q, self.c)
+        self.sends.append(whole)
+        return whole.wait_recv
+
+    def drain(self):
+        for copy in self.sends + list(self.flying.values()):
+            copy.wait_send()
+        for copy in self.stores.values():
+            copy.wait()
+
+
+class Layer:
+    def __init__(self, packed, per, n):
+        self.per = per
+        self.n = n
+        self.rows = 2 * per
+        self.packed = packed
+        self.value_rows = per // 2 if self.packed else per
+        self.message = per + self.value_rows
+        self.total = n * per
+        self.block = 256
+        self.gains = (0, 1) if packed else (2, 3)
+
+    def attach(self, env, refs, sources, weights, results):
+        self.b = refs
+        self.held = weights
+        self.results = results
+        self.right_waits, self.left_waits, self.line_waits = {}, {}, {}
+        self.loads = {}
+        for number, (source, weight) in enumerate(zip(sources, weights, strict=True)):
+            copy = pltpu.make_async_copy(source, weight, env.sem())
+            copy.start()
+            self.loads[number] = copy
+
+    def weight(self, number):
+        if number in self.loads:
+            self.loads.pop(number).wait()
+        return self.held[number]
+
+    def buffers(self):
+        r, t, n = self.rows, self.total, self.n
+        vr, m = self.value_rows, self.message
+        table = dict(
+            normed=((r, 1024), BF),
+            s1=((n, m, 128), BF),
+            r1=((n, m, 128), BF),
+            qa=((t, 128), BF),
+            kb=((t, 128), BF),
+            va=((t, 128), BF),
+            mixp=((t, 128), F32),
+            lse=((t, 128), F32),
+            s2=((n, vr, 128), BF),
+            r2=((n, vr, 128), BF),
+            mixl=((r, 512), BF),
+            mid=((r, 1024), F32),
+            nm=((r, 1024), BF),
+            gp=((r, 2048), BF),
+            act=((r, 2048), BF),
+            e=((r, 1024), F32),
+            el=((r, 1024), BF),
+            gb=((r, 2048), BF),
+            gm=((r, 1024), F32),
+            al=((r, 1024), BF),
+            s6=((n, vr, 128), BF),
+            r6=((n, vr, 128), BF),
+            gx=((t, 128), BF),
+            dk=((t, 128), F32),
+            dv=((t, 128), F32),
+            s7=((n, m, 128), BF),
+            r7=((n, m, 128), BF),
+            dp=((r, 1536), BF),
+            acc=((r, 1024), F32),
+            ps=((2, 4, r, 256), BF),
+            pr=((2, 4, r, 256), BF),
+            fg=((4, r, 6144), BF),
+            ds=((4, r, 1024), BF),
+            dg=((4, r, 1024), BF),
+            sb=((4, 64, 6144), BF),
+            rb=((3, 64, 6144), BF),
+        )
+        if not self.packed:
+            table.update(
+                x=((r, 1024), BF),
+                same=((t, t), F32),
+                lab=((t, 128), BF),
+                hot=((2, self.per, 64), BF),
+                labs=((r, 128), F32),
+            )
+        return table
+
+    def gain(self, env, which):
+        row = self.gains[which]
+        return env.b.vecs[row : row + 1, :]
+
+    def pack(self, tile):
+        if not self.packed:
+            return tile
+        half = self.per // 2
+        return jnp.where(low_lanes(half), tile[:half], swap_halves(tile[half:]))
+
+    def send_pairs(self, store, tile_of):
+        for seq in range(2):
+            for j in range(4):
+                tile = tile_of(seq, j)
+                store(8 * seq + 2 * j, self.pack(tile))
+                store(8 * seq + 2 * j + 1, self.pack(swap_halves(tile)))
+
+    def join_pairs(self, tile_a, tile_b):
+        vr = self.value_rows
+        low = low_lanes(vr)
+        first = jnp.where(low, tile_a, swap_halves(tile_b))
+        if not self.packed:
+            return [first]
+        return [first, jnp.where(low, swap_halves(tile_a), tile_b)]
+
+    def project(self, env):
+        hidden = self.b.x[...].astype(F32)
+        normed = (hidden * inverse_rms(hidden) * self.gain(env, 0)).astype(BF)
+        self.b.normed[...] = normed
+        weight = self.weight(QKV)
+        queries, keys, values = (dot(normed, weight[part]) for part in range(3))
+        send = self.b.s1
+        per = self.per
+        low = low_lanes(per)
+        for seq in range(2):
+            rows = slice(seq * per, (seq + 1) * per)
+            for j in range(4):
+                cols = slice(128 * j, 128 * j + 128)
+                qt, kt, vt = queries[rows, cols], keys[rows, cols], values[rows, cols]
+                pair = 8 * seq + 2 * j
+                send[pair, 0:per] = jnp.where(low, qt, swap_halves(kt)).astype(BF)
+                send[pair + 1, 0:per] = jnp.where(low, swap_halves(qt), kt).astype(BF)
+                va, vb = vt, swap_halves(vt)
+                if self.packed:
+                    va, vb = self.pack(va), self.pack(vb)
+                else:
+                    labels = self.b.labs[rows, :]
+                    va, vb = jnp.where(low, va, labels), jnp.where(low, vb, labels)
+                send[pair, per:] = va.astype(BF)
+                send[pair + 1, per:] = vb.astype(BF)
+        self.wait1 = env.exchange(send, self.b.r1)
+
+    def unpack(self, env):
+        recv = self.b.r1
+        qa, kb, va = self.b.qa, self.b.kb, self.b.va
+        per, vr = self.per, self.value_rows
+        low, low_v = low_lanes(per), low_lanes(vr)
+        zero = jnp.zeros((per, 128), F32)
+        zero_v = jnp.zeros((vr, 128), F32)
+        for i in range(self.n):
+            both = recv[i, 0:per].astype(F32)
+            qa[i * per : (i + 1) * per] = jnp.where(low, both * 0.125, zero).astype(BF)
+            kb[i * per : (i + 1) * per] = swap_halves(both).astype(BF)
+            tile = recv[i, per:].astype(F32)
+            va[i * per : i * per + vr] = jnp.where(low_v, tile, zero_v).astype(BF)
+            if self.packed:
+                va[i * per + vr : (i + 1) * per] = jnp.where(low_v, swap_halves(tile), zero_v).astype(BF)
+            else:
+                self.b.lab[i * per : (i + 1) * per] = jnp.where(low_v, zero_v, tile).astype(BF)
+        if not self.packed:
+            labels = self.b.lab[...]
+            self.b.same[...] = dot_t(labels, labels)
+
+    def allowed(self, env, start, stop):
+        size = stop - start
+        rows = lax.broadcasted_iota(jnp.int32, (size, stop), 0) + start
+        keys = lax.broadcasted_iota(jnp.int32, (size, stop), 1)
+        ok = keys <= rows
+        if self.packed:
+            segments = env.b.segments[pl.ds(lax.div(env.s, 8), 1), :]
+            row = (lax.broadcasted_iota(jnp.int32, (size, 1), 0) + start).astype(F32)
+            opening = jnp.zeros((size, 1), F32)
+            for label in range(1, 4):
+                edge = jnp.sum((segments < label).astype(F32), axis=1, keepdims=True)
+                opening = jnp.where(row >= edge, jnp.maximum(opening, edge), opening)
+            return ok & (keys >= opening.astype(jnp.int32))
+        return ok & (self.b.same[start:stop, 0:stop] > 0.5)
+
+    def attend(self, env):
+        self.wait1()
+        self.unpack(env)
+        qa, kb, va = self.b.qa, self.b.kb, self.b.va
+        mixp, lse = self.b.mixp, self.b.lse
+        for start in range(0, self.total, self.block):
+            stop = start + self.block
+            scores = dot_t(qa[start:stop], kb[0:stop])
+            scores = jnp.where(self.allowed(env, start, stop), scores, NEGATIVE)
+            highest = jnp.max(scores, axis=1, keepdims=True)
+            weights = jnp.exp(scores - highest)
+            totals = jnp.sum(weights, axis=1, keepdims=True)
+            mixp[start:stop] = dot(weights.astype(BF), va[0:stop]) / totals
+            lse[start:stop] = jnp.broadcast_to(highest + jnp.log(totals), (self.block, 128))
+        send = self.b.s2
+        for i in range(self.n):
+            send[i] = self.pack(mixp[i * self.per : (i + 1) * self.per]).astype(BF)
+        self.wait2 = env.exchange(send, self.b.r2)
+
+    def gather_heads(self, recv, row0, put):
+        per, vr = self.per, self.value_rows
+        for seq in range(2):
+            for j in range(4):
+                pair = 8 * seq + 2 * j
+                tiles = self.join_pairs(
+                    recv[pair, row0:].astype(F32), recv[pair + 1, row0:].astype(F32)
+                )
+                for number, tile in enumerate(tiles):
+                    begin = seq * per + number * vr
+                    put(slice(begin, begin + vr), slice(128 * j, 128 * j + 128), tile)
+
+    def feed(self, env, finish):
+        self.wait2()
+        mixl = self.b.mixl
+
+        def put(rows, cols, tile):
+            mixl[rows, cols] = tile.astype(BF)
+
+        self.gather_heads(self.b.r2, 0, put)
+        out = self.weight(OUT)
+        mid = self.b.mid
+        hidden = self.b.x
+        mixed = mixl[...]
+
+        def sink(number, value):
+            cols = slice(256 * number, 256 * number + 256)
+            mid[:, cols] = value + hidden[:, cols].astype(F32)
+
+        env.core_sum(
+            self,
+            0,
+            lambda number: dot(mixed, out[:, 256 * number : 256 * number + 256]),
+            sink,
+        )
+        middle = mid[...]
+        normed = (middle * inverse_rms(middle) * self.gain(env, 1)).astype(BF)
+        self.b.nm[...] = normed
+        up = self.weight(UP)
+        act, slope = self.b.act, self.b.gp
+        for number in range(4):
+            cols = slice(512 * number, 512 * number + 512)
+            before = dot(normed, up[:, cols])
+            square = before * before
+            bent = jnp.tanh(0.7978845608028654 * before * (1.0 + 0.044715 * square))
+            half = 0.5 * (1.0 + bent)
+            act[:, cols] = (before * half).astype(BF)
+            slope[:, cols] = (
+                half
+                + 0.5 * before * (1.0 - bent * bent) * (0.7978845608028654 + 0.1070322243 * square)
+            ).astype(BF)
+        down = self.weight(DOWN)
+        env.core_sum(
+            self,
+            1,
+            lambda number: dot(act[...], down[:, 256 * number : 256 * number + 256]),
+            finish,
+        )
+
+    def back_feed(self, env):
+        grad_low = self.b.e[...].astype(BF)
+        self.b.el[...] = grad_low
+        down, up, out = self.weight(DOWN), self.weight(UP), self.weight(OUT)
+        gb, slope = self.b.gb, self.b.gp
+        for number in range(4):
+            cols = slice(512 * number, 512 * number + 512)
+            grad = dot_t(grad_low, down[cols, :])
+            gb[:, cols] = (grad * slope[:, cols].astype(F32)).astype(BF)
+        acc = self.b.acc
+
+        def sink(number, value):
+            acc[:, 256 * number : 256 * number + 256] = value
+
+        env.core_sum(
+            self,
+            0,
+            lambda number: dot_t(gb[...], up[256 * number : 256 * number + 256, :]),
+            sink,
+        )
+        grad_mid, grad_gain = norm_back(acc[...], self.b.mid[...], self.gain(env, 1))
+        row = self.gains[1]
+        env.b.vg[row : row + 1, :] = grad_gain
+        self.b.gm[...] = grad_mid
+        along = (self.b.e[...] + grad_mid).astype(BF)
+        self.b.al[...] = along
+        grad_mixed = dot_t(along, out[...])
+        send = self.b.s6
+        per = self.per
+
+        def store(pair, tile):
+            send[pair] = tile.astype(BF)
+
+        self.send_pairs(
+            store,
+            lambda seq, j: grad_mixed[seq * per : (seq + 1) * per, 128 * j : 128 * j + 128],
+        )
+        self.wait6 = env.exchange(send, self.b.r6)
+
+    def back_attend(self, env):
+        self.wait6()
+        recv, gx = self.b.r6, self.b.gx
+        per, vr = self.per, self.value_rows
+        low_v = low_lanes(vr)
+        zero_v = jnp.zeros((vr, 128), F32)
+        for i in range(self.n):
+            tile = recv[i].astype(F32)
+            gx[i * per : i * per + vr] = jnp.where(low_v, tile, zero_v).astype(BF)
+            if self.packed:
+                gx[i * per + vr : (i + 1) * per] = jnp.where(low_v, swap_halves(tile), zero_v).astype(BF)
+        qa, kb, va = self.b.qa, self.b.kb, self.b.va
+        mixp, lse = self.b.mixp, self.b.lse
+        dk, dv = self.b.dk, self.b.dv
+        dk[...] = jnp.zeros_like(dk)
+        dv[...] = jnp.zeros_like(dv)
+        dq = {}
+        for start in range(0, self.total, self.block):
+            stop = start + self.block
+            query, grad = qa[start:stop], gx[start:stop]
+            scores = dot_t(query, kb[0:stop])
+            scores = jnp.where(self.allowed(env, start, stop), scores, NEGATIVE)
+            probs = jnp.exp(scores - lse[start:stop, 0:1])
+            offsets = jnp.sum(grad.astype(F32) * mixp[start:stop], axis=1, keepdims=True)
+            slopes = (probs * (dot_t(grad, va[0:stop]) - offsets)).astype(BF)
+            mixp[start:stop] = dot(slopes, kb[0:stop])
+            dk[0:stop] += dot_l(slopes, query)
+            dv[0:stop] += dot_l(probs.astype(BF), grad)
+        send = self.b.s7
+        low = low_lanes(per)
+        for i in range(self.n):
+            rows = slice(i * per, (i + 1) * per)
+            send[i, 0:per] = jnp.where(low, mixp[rows] * 0.125, swap_halves(dk[rows])).astype(BF)
+            send[i, per:] = self.pack(dv[rows]).astype(BF)
+        self.wait7 = env.exchange(send, self.b.r7)
+
+    def back_project(self, env, finish):
+        self.wait7()
+        recv, dp = self.b.r7, self.b.dp
+        per = self.per
+        low = low_lanes(per)
+        for seq in range(2):
+            rows = slice(seq * per, (seq + 1) * per)
+            for j in range(4):
+                pair = 8 * seq + 2 * j
+                one, two = recv[pair, 0:per].astype(F32), recv[pair + 1, 0:per].astype(F32)
+                dp[rows, 128 * j : 128 * j + 128] = jnp.where(low, one, swap_halves(two)).astype(BF)
+                dp[rows, 512 + 128 * j : 640 + 128 * j] = jnp.where(low, swap_halves(one), two).astype(BF)
+
+        def put(rows, cols, tile):
+            dp[rows, 1024 + cols.start : 1024 + cols.stop] = tile.astype(BF)
+
+        self.gather_heads(recv, per, put)
+        weight = self.weight(QKV)
+        acc = self.b.acc
+
+        def chunk(number):
+            rows = slice(256 * number, 256 * number + 256)
+            total = dot_t(dp[:, 0:512], weight[0, rows, :])
+            total += dot_t(dp[:, 512:1024], weight[1, rows, :])
+            return total + dot_t(dp[:, 1024:1536], weight[2, rows, :])
+
+        def sink(number, value):
+            acc[:, 256 * number : 256 * number + 256] = value
+
+        env.core_sum(self, 1, chunk, sink)
+        grad_hidden, grad_gain = norm_back(
+            acc[...], self.b.x[...].astype(F32), self.gain(env, 0)
+        )
+        row = self.gains[0]
+        env.b.vg[row : row + 1, :] = grad_gain
+        finish(self.b.gm[...] + grad_hidden)
+
+    def parts(self, env, which):
+        b = self.b
+        left = (b.normed, b.al, b.nm, b.el)[which]
+        right = (b.dp, b.mixl, b.gb, b.act)[which]
+        return left, right
+
+    def share(self, env, which):
+        self.share_right(env, which)
+        self.share_left(env, which)
+
+    def share_right(self, env, which):
+        begin, size = COLS[which]
+        _, right = self.parts(env, which)
+        fg = self.b.fg
+        cols = pl.ds(begin, size)
+        fg[pl.ds(env.q, 1), :, begin : begin + size] = right[...][None]
+        mine = fg.at[env.q, :, cols]
+        self.right_waits[which] = env.plane_send(
+            lambda other: mine, mine, fg.at[pl.ds(0, 3), :, cols]
+        )
+
+    def share_left(self, env, which):
+        left, _ = self.parts(env, which)
+        ds, dg = self.b.ds, self.b.dg
+        low = low_lanes(self.rows)
+        begin = 256 * which
+        for a in range(2):
+            tiles = [
+                left[:, 128 * (2 * z + a) : 128 * (2 * z + a) + 128].astype(F32) for z in range(4)
+            ]
+            for two in range(2):
+                even, odd = tiles[2 * two], tiles[2 * two + 1]
+                at = begin + 128 * two
+                ds[2 * a, :, at : at + 128] = jnp.where(low, even, swap_halves(odd)).astype(BF)
+                ds[2 * a + 1, :, at : at + 128] = jnp.where(low, swap_halves(even), odd).astype(BF)
+        cols = pl.ds(begin, 256)
+        dg[pl.ds(env.q, 1), :, begin : begin + 256] = ds[pl.ds(env.q, 1), :, begin : begin + 256]
+        self.left_waits[which] = env.plane_send(
+            lambda other: ds.at[other, :, cols],
+            dg.at[env.q, :, cols],
+            dg.at[pl.ds(0, 3), :, cols],
+        )
+
+    def multiply(self, env, which):
+        self.right_waits[which]()
+        self.left_waits[which]()
+        begin, size = COLS[which]
+        fg, dg, sb, rb = self.b.fg, self.b.dg, self.b.sb, self.b.rb
+        rows = 4 * self.rows
+        left = dg[:, :, 256 * which : 256 * which + 256].reshape(rows, 256)
+        for at in range(begin, begin + size, 512):
+            right = fg[:, :, at : at + 512].reshape(rows, 512)
+            product = dot_l(left, right)
+            for z in range(4):
+                sb[z, :, at : at + 512] = product[64 * z : 64 * z + 64].astype(BF)
+        cols = pl.ds(begin, size)
+        self.line_waits[which] = env.line_send(
+            lambda other: sb.at[other, :, cols],
+            lambda step: rb.at[step - 1, :, cols],
+            rb.at[:, :, cols],
+        )
+
+    def collect(self, env, which):
+        self.line_waits[which]()
+        begin, size = COLS[which]
+        sb, rb = self.b.sb, self.b.rb
+        result = self.results[which]
+        for at in range(0, size, 512):
+            cols = slice(begin + at, begin + at + 512)
+            slot = env.stored % 4
+            env.stored += 1
+            if slot in env.stores:
+                env.stores.pop(slot).wait()
+            total = sb[pl.ds(env.z, 1), :, cols].astype(F32)
+            for step in range(1, 4):
+                total = total + rb[step - 1 : step, :, cols].astype(F32)
+            stage = env.b.stage
+            stage[slot] = total[0]
+            target = result.at[at // 512] if which == 0 else result.at[:, pl.ds(at, 512)]
+            copy = pltpu.make_async_copy(stage.at[slot], target, env.sem())
+            copy.start()
+            env.stores[slot] = copy
+
+
+def pick_rows(env, dense, routed):
+    hot, labs, first = routed.b.hot, routed.b.labs, env.b.output
+    group, slots = dense.per, routed.per
+    base = env.s * group
+    for seq in range(2):
+        listed = env.b.routed[seq : seq + 1, :]
+        places = listed.shape[1]
+        place = lax.broadcasted_iota(jnp.int32, (group, places), 0) + base
+        here = (place == listed).astype(F32).astype(BF)
+        before = jnp.sum((listed < base).astype(F32), axis=1, keepdims=True).astype(jnp.int32)
+        number = lax.broadcasted_iota(jnp.int32, (slots, places), 1) - before
+        slot = lax.broadcasted_iota(jnp.int32, (slots, places), 0)
+        mine = (number == slot).astype(F32).astype(BF)
+        table = dot_t(mine, here).astype(BF)
+        hot[seq] = table
+        segments = env.b.segments[seq : seq + 1, :]
+        row = (lax.broadcasted_iota(jnp.int32, (group, 1), 0) + base).astype(F32)
+        label = jnp.zeros((group, 1), F32)
+        for number in range(1, 4):
+            edge = jnp.sum((segments < number).astype(F32), axis=1, keepdims=True)
+            label = label + (row >= edge).astype(F32)
+        lane = lax.broadcasted_iota(jnp.int32, (group, 128), 1)
+        one_hot = (lane == label.astype(jnp.int32) + 64).astype(F32).astype(BF)
+        labs[seq * slots : (seq + 1) * slots, :] = dot(table, one_hot)
+        rows = first[seq * group : (seq + 1) * group, :].astype(BF)
+        routed.b.x[seq * slots : (seq + 1) * slots, :] = dot(table, rows).astype(BF)
+
+
+def restore(env, dense, routed, sent, seq):
+    slots = routed.per
+    return dot_l(routed.b.hot[seq], sent[seq * slots : (seq + 1) * slots])
+
+
+def gate_rows(env, dense, routed):
+    group, slots = dense.per, routed.per
+    sent = routed.b.acc[...].astype(BF)
+    router = env.b.vecs[4:5, :]
+    grad_router = jnp.zeros((1, 1024), F32)
+    for seq in range(2):
+        rows = slice(seq * group, (seq + 1) * group)
+        first = env.b.output[rows, :]
+        returned = restore(env, dense, routed, sent, seq)
+        gate = jax.nn.sigmoid(jnp.sum(first * router, axis=1, keepdims=True))
+        env.b.output[rows, :] = first + gate * returned
+        grad = env.b.cotangent[rows, :].astype(F32)
+        low = (gate * grad).astype(BF)
+        routed.b.e[seq * slots : (seq + 1) * slots, :] = dot(routed.b.hot[seq], low)
+        logit = jnp.sum(grad * returned, axis=1, keepdims=True) * gate * (1.0 - gate)
+        grad_router = grad_router + jnp.sum(logit * first, axis=0, keepdims=True)
+        dense.b.e[rows, :] = grad + logit * router
+    env.b.vg[4:5, :] = grad_router
+
+
+def share_vectors(env):
+    vg, sv, rv = env.b.vg, env.b.sv, env.b.rv
+    for number in range(env.n):
+        tile = vg[:, 128 * (number // 2) : 128 * (number // 2) + 128]
+        sv[number] = swap_halves(tile) if number % 2 else tile
+    return env.exchange(sv, rv)
+
+
+def sum_vectors(env, wait):
+    wait()
+    total = env.b.rv[0]
+    for number in range(1, env.n):
+        total = total + env.b.rv[number]
+    env.b.gvec[...] = total
+
+
+QKV, OUT, UP, DOWN = range(4)
+SHAPES = ((3, 1024, 512), (512, 1024), (1024, 2048), (2048, 1024))
+GRADS = ((3, 64, 512), (64, 512), (64, 2048), (64, 2048))
+
+
+def whole_step(env, dense, routed):
+    env.greet()
+    env.b.vg[...] = jnp.zeros_like(env.b.vg)
+    dense.project(env)
+    dense.attend(env)
+    mid_d, first = dense.b.mid, env.b.output
+
+    def finish_dense(number, value):
+        cols = slice(256 * number, 256 * number + 256)
+        first[:, cols] = mid_d[:, cols] + value
+
+    dense.feed(env, finish_dense)
+    pick_rows(env, dense, routed)
+    routed.project(env)
+    routed.attend(env)
+    mid_r, x_r, sent = routed.b.mid, routed.b.x, routed.b.acc
+
+    def finish_routed(number, value):
+        cols = slice(256 * number, 256 * number + 256)
+        sent[:, cols] = mid_r[:, cols] - x_r[:, cols].astype(F32) + value
+
+    routed.feed(env, finish_routed)
+    gate_rows(env, dense, routed)
+    routed.back_feed(env)
+    for which in (3, 2, 1):
+        routed.share(env, which)
+    routed.back_attend(env)
+    for which in (3, 2, 1):
+        routed.multiply(env, which)
+
+    def finish_back(branch):
+        low = branch.astype(BF)
+        for seq in range(2):
+            rows = slice(seq * dense.per, (seq + 1) * dense.per)
+            dense.b.e[rows, :] += restore(env, dense, routed, low, seq)
+
+    routed.back_project(env, finish_back)
+    routed.share(env, 0)
+    dense.back_feed(env)
+    for which in (3, 2, 1):
+        dense.share(env, which)
+    routed.multiply(env, 0)
+    dense.back_attend(env)
+    for which in (3, 2, 1):
+        dense.multiply(env, which)
+
+    def finish_tokens(branch):
+        env.b.grad_tokens[...] = dense.b.e[...] + branch
+
+    dense.back_project(env, finish_tokens)
+    dense.share(env, 0)
+    wait = share_vectors(env)
+    for which in (3, 2, 1, 0):
+        routed.collect(env, which)
+    dense.multiply(env, 0)
+    for which in (3, 2, 1, 0):
+        dense.collect(env, which)
+    sum_vectors(env, wait)
+    env.drain()
+
+
+def fused(group, tokens, cotangent, segments, routed_places, vecs, weights):
+    n = lax.axis_size("seq")
+    rows = 2 * group
+    dense, routed = Layer(True, group, n), Layer(False, group // 4, n)
+    wide = ((rows, 1024), F32)
+    common = dict(
+        stage=((4, 64, 512), F32),
+        vg=((8, 1024), F32),
+        sv=((n, 8, 128), F32),
+        rv=((n, 8, 128), F32),
+    )
+    groups = (dense.buffers(), routed.buffers(), common)
+    scratch = [spec for table in groups for spec in table.values()]
+
+    def kernel(*refs):
+        refs = list(refs)
+
+        def take(count):
+            taken = refs[:count]
+            del refs[:count]
+            return taken
+
+        x, cotangent_ref, segments_ref, routed_ref, vecs_ref = take(5)
+        sources = take(8)
+        output, grad_tokens, gvec = take(3)
+        results = take(8)
+        held = take(8)
+        dense_refs, routed_refs, common_refs = (
+            types.SimpleNamespace(**dict(zip(table, take(len(table)), strict=True))) for table in groups
+        )
+        dense_refs.x = x
+        common_refs.cotangent = cotangent_ref
+        common_refs.segments = segments_ref
+        common_refs.routed = routed_ref
+        common_refs.vecs = vecs_ref
+        common_refs.output = output
+        common_refs.grad_tokens = grad_tokens
+        common_refs.gvec = gvec
+        env = Env(common_refs, refs[0], n)
+        dense.attach(env, dense_refs, sources[:4], held[:4], results[:4])
+        routed.attach(env, routed_refs, sources[4:], held[4:], results[4:])
+        whole_step(env, dense, routed)
+
+    vmem = pl.BlockSpec(memory_space=pltpu.VMEM)
+    hbm = pl.BlockSpec(memory_space=pl.ANY)
+    outs = [wide, wide, ((8, 128), F32)] + [(shape, F32) for shape in GRADS * 2]
+    results = pl.pallas_call(
+        kernel,
+        out_shape=[jax.ShapeDtypeStruct(*spec) for spec in outs],
+        in_specs=[vmem] * 5 + [hbm] * 8,
+        out_specs=[vmem] * 3 + [hbm] * 8,
+        scratch_shapes=[pltpu.VMEM(shape, BF) for shape in SHAPES * 2]
+        + [pltpu.VMEM(*spec) for spec in scratch]
+        + [pltpu.SemaphoreType.DMA((192,))],
+        compiler_params=pltpu.CompilerParams(
+            collective_id=0, has_side_effects=True, vmem_limit_bytes=LIMIT
+        ),
+    )(tokens, cotangent, segments, routed_places, vecs, *weights)
+    return results[0], results[1], results[2], results[3:7], results[7:]
+
+
+def on_device_fused(
+    tokens,
+    segments,
+    routed,
+    router,
+    dense_attn_gain,
+    dense_qkv,
+    dense_out,
+    dense_mlp_gain,
+    dense_up,
+    dense_down,
+    routed_attn_gain,
+    routed_qkv,
+    routed_out,
+    routed_mlp_gain,
+    routed_up,
+    routed_down,
+    cotangent,
+):
+    group, seqs, width = tokens.shape
+    zeros = jnp.zeros_like(router)
+    vecs = jnp.stack(
+        (dense_attn_gain, dense_mlp_gain, routed_attn_gain, routed_mlp_gain, router, zeros, zeros, zeros)
+    ).astype(F32)
+
+    def rows_of(array):
+        return jnp.transpose(array, (1, 0, 2)).reshape(seqs * group, width)
+
+    output, grad_tokens, gvec, dense_grads, routed_grads = fused(
+        group,
+        rows_of(tokens),
+        rows_of(cotangent),
+        segments,
+        routed,
+        vecs,
+        (
+            jnp.transpose(dense_qkv, (1, 0, 2)),
+            dense_out,
+            dense_up,
+            dense_down,
+            jnp.transpose(routed_qkv, (1, 0, 2)),
+            routed_out,
+            routed_up,
+            routed_down,
+        ),
+    )
+
+    def back(array):
+        return jnp.transpose(array.reshape(seqs, group, width), (1, 0, 2))
+
+    def vector(row):
+        return gvec[row, 0:64]
+
+    def weights_of(grads, first, second):
+        return (
+            vector(first),
+            jnp.transpose(grads[QKV], (1, 0, 2)),
+            jnp.transpose(grads[OUT]),
+            vector(second),
+            grads[UP],
+            jnp.transpose(grads[DOWN]),
+        )
+
+    return (
+        (back(output), back(grad_tokens))
+        + weights_of(dense_grads, 0, 1)
+        + weights_of(routed_grads, 2, 3)
+        + (vector(4),)
+    )
+
+
 def solution(mesh):
     in_specs = (
         P("seq", None, None),
@@ -467,6 +1338,10 @@
         P("mp", "seq"),
         P("seq"),
     )
+    seq_size = mesh.shape["seq"]
+    pairs = 2 * (16 // mesh.shape["mp"])
+    body = on_device_fused if seq_size == pairs else on_device
+
     return jax.shard_map(
-        on_device, mesh=mesh, in_specs=in_specs, out_specs=out_specs, check_vma=False
-    )
+        body, mesh=mesh, in_specs=in_specs, out_specs=out_specs, check_vma=False
+    )

time: 2070 us -> 237 us (0.11)
  waiting for transfers between devices: 1210 us -> 0 us
  blocking collectives: 427 us -> 0 us
  Pallas kernels: 0 us -> 213 us
  local copies, waits for them, and re-layouts: 200 us -> 20.4 us
  matrix products: 135 us -> 0 us
  other arithmetic: 66.1 us -> 0.62 us
    reduce_scatter x8 -> x0, waiting for transfers between devices: 1070 us -> none  [the longest x1 183 us: on_device(): lax.psum_scatter(routed_grads[5], 'seq', scatter_dimension=1, tiled=True)]
    all_gather x8 -> x0, blocking collectives: 355 us -> none  [the longest x2 90.5 us: attend_backward(): lax.all_gather(jnp.transpose(log_sum, (2, 0, 1)), 'seq', axis=0, tiled=True)]
    pallas_call x0 -> x1, Pallas kernels: none -> 213 us  [fused(): pl.pallas_call(kernel, out_shape=[jax.ShapeDtypeStruct(*spec) for spec in...]
    dot_general x50 -> x0, matrix products: 135 us -> none  [the longest x3 10.8 us: advance(): jnp.einsum('shqk,kshe->qshe', slopes, key_block, preferred_element_type=j...]
    all_gather x4 -> x0, waiting for transfers between devices: 87.6 us -> none  [the longest x1 58.6 us: attend_forward(): value_piece = lax.all_gather(value_rows, 'seq', axis=0, tiled=True)]
    gather x50 -> x0, local copies, waits for them, and re-layouts: 85.9 us -> none  [the longest x15 51.1 us: key_mask(): key_labels = jnp.take_along_axis(label_rows, key_places, axis=0)]
    unnamed x1 -> x0, blocking collectives: 72.1 us -> none
    psum x7 -> x0, waiting for transfers between devices: 56 us -> none  [model_sum(): return lax.psum(operand, 'mp')]
  transfers between devices with their start and end apart: 19 -> 0, of which waited for: 13 -> 0; matrix products, arithmetic and copies ran while one was open for 9% -> 0% of each run, Pallas kernels for 0% -> 0%
where the time goes in v1:
time: 237 us; the launch traced here: 235 us
  Pallas kernels  213 us (90%)
  local copies, waits for them, and re-layouts  20.4 us (9%)
    pallas_call x1, Pallas kernels, fused(): pl.pallas_call(kernel, out_shape=[jax.ShapeDtypeStruct(*spec) for spec in...  213 us
    unnamed x18, local copies, waits for them, and re-layouts  9.01 us

profile of v1, /device:TPU:0, one launch (start us, length us, event | category | flops | bytes accessed | tf_op | source)
XLA Modules:
  0.0 235.0 jit_solution(10130938594675445016)
XLA Ops:
  0.6 0.7 stack.25
  1.3 0.7 stack.21
  2.0 0.7 stack.22
  2.7 0.7 stack.23
  3.4 0.7 stack.24
  4.1 0.1 stack.27
  4.2 0.6 convert_element_type.3.refs_4_
  4.8 1.7 copy.32
  6.5 1.7 copy.33
  8.2 213.2 %shard_map.280 = (f32[128,1024]{1,0:T(8,128)}, f32[128,1024]{1,0:T(8,128)}, f32[8,128]{1,0:T(8,128)}, f32[3,64,512]{2,1,0:T(8,128)}, f32[64,512]{1,0:T(8,128)}, ...) custom-call(bf16[128,1024]{1,0:T(8,128)(2,1)} %bitcast.30, ...), custom_call_target="tpu_custom_call" | custom-call | tf_op jit(solution)/shard_map/pallas_call | solution.py:1218
  221.4 0.0 copy-start.2
  221.4 0.0 copy-start.3
  221.4 0.0 copy-start.4
  221.4 0.0 copy-start.1
  221.4 0.0 copy-start
  221.5 3.1 %copy_bitcast_fusion = (f32[64,2,1024]{2,1,0:T(2,128)}, f32[64,2,1024]{2,1,0:T(2,128)}) fusion(f32[2,64,1024]{2,1,0:T(8,128)} %bitcast.35, f32[2,64,1024]{2,1,0:T(8,128)} %bitcast.34), kind=kLoop, calls=%fused_computation | loop fusion | bytes 2097152 | tf_op jit(solution)/shard_map/transpose | solution.py:1281
  224.6 1.4 slice_bitcast_fusion
  226.0 1.8 copy.46
  227.7 1.6 copy.47
  229.3 1.9 copy.48
  231.2 0.0 copy-done.2
  231.2 0.8 copy.49
  232.0 0.0 copy-done.3
  232.0 0.7 copy.50
  232.7 0.0 copy-done.4
  232.7 0.7 copy.51
  233.4 0.0 copy-done.1
  233.4 0.8 copy.52
  234.2 0.0 copy-done
  234.2 0.8 copy.53
  (2 shorter events, 0.0 us)
Async XLA Ops:
  221.4 9.8 %copy-start.2 = (f32[64,2048]{1,0:T(8,128)S(1)}, f32[64,2048]{1,0:T(8,128)}, u32[]{:S(2)}) copy-start(f32[64,2048]{1,0:T(8,128)} %get-tuple-element.32) | copy-start | bytes 1572868
  221.4 10.5 %copy-start.3 = (f32[3,64,512]{2,1,0:T(8,128)S(1)}, f32[3,64,512]{2,1,0:T(8,128)}, u32[]{:S(2)}) copy-start(f32[3,64,512]{2,1,0:T(8,128)} %get-tuple-element.33) | copy-start | bytes 1179652
  221.4 11.3 %copy-start.4 = (f32[64,512]{1,0:T(8,128)S(1)}, f32[64,512]{1,0:T(8,128)}, u32[]{:S(2)}) copy-start(f32[64,512]{1,0:T(8,128)} %get-tuple-element.34) | copy-start | bytes 393220
  221.4 11.9 %copy-start.1 = (f32[64,2048]{1,0:T(8,128)S(1)}, f32[64,2048]{1,0:T(8,128)}, u32[]{:S(2)}) copy-start(f32[64,2048]{1,0:T(8,128)} %get-tuple-element.71) | copy-start | bytes 1572868
  221.4 12.7 %copy-start = (f32[64,2048]{1,0:T(8,128)S(1)}, f32[64,2048]{1,0:T(8,128)}, u32[]{:S(2)}) copy-start(f32[64,2048]{1,0:T(8,128)} %get-tuple-element.36) | copy-start | bytes 1572868

commit v2 on v1

--- a/solution.py
+++ b/solution.py
@@ -437,7 +437,10 @@
 LIMIT = 63 * 1024 * 1024
 F32 = jnp.float32
 MESH = pl.DeviceIdType.MESH
-COLS = ((0, 1536), (1536, 512), (2048, 2048), (4096, 2048))
+WIDTHS = (384, 128, 512, 512)
+BEGINS = (0, 384, 512, 1024)
+SIZES = (1536, 512, 2048, 2048)
+COLS = (None, (0, 512), (512, 2048), (2560, 2048))
 
 
 def dot(a, b):
@@ -487,10 +490,18 @@
         self.c = lax.axis_index("mp")
         self.q = lax.rem(self.s, 4)
         self.z = lax.div(self.s, 4)
+        high = lax.div(self.z, 2)
+        self.near = self.z + 1 - 2 * lax.rem(self.z, 2)
+        self.across = 2 - high
+        self.far = 3 - 3 * high
+        self.middle = lax.rem(self.z + high, 2) == 1
 
     def sem(self):
         self.count += 1
         return self.sems.at[self.count - 1]
+
+    def vector(self, number):
+        return self.b.vectors[number][...].astype(F32).reshape(1, 1024)
 
     def greet(self):
         barrier = pltpu.get_barrier_semaphore()
@@ -586,6 +597,57 @@
         self.sends.append(whole)
         return whole.wait_recv
 
+    def line_reduce(self, blocks, slots):
+        self.meet()
+        receive = [self.sem() for _ in range(4)]
+        send = [self.sem() for _ in range(3)]
+
+        def copy(block, slot, way, z):
+            return self.remote(
+                blocks.at[block], slots.at[slot], send[way], receive[slot], z * 4 + self.q, self.c
+            )
+
+        copy(self.near, 0, 0, self.near).start()
+
+        @pl.when(self.middle)
+        def _():
+            copy(self.across, 1, 1, self.across).start()
+
+        @pl.when(jnp.logical_not(self.middle))
+        def _():
+            copy(self.far, 3, 2, self.near).start()
+            copy(self.across, 2, 1, self.across).start()
+
+        self.sends += [copy(0, 0, way, self.near) for way in range(3)]
+
+        def arrived():
+            copy(0, 3, 0, self.near).wait_recv()
+
+        def pass_on():
+            copy(self.far, 1, 2, self.far).start()
+
+        def finish():
+            copy(0, 0, 0, self.near).wait_recv()
+            copy(0, 1, 0, self.near).wait_recv()
+
+            @pl.when(self.middle)
+            def _():
+                copy(0, 2, 0, self.near).wait_recv()
+
+        return arrived, pass_on, finish
+
+    def store(self, result, which, at, fill):
+        slot = self.stored % 4
+        self.stored += 1
+        if slot in self.stores:
+            self.stores.pop(slot).wait()
+        stage = self.b.stage.at[slot]
+        fill(stage)
+        target = result.at[at // 512] if which == 0 else result.at[:, pl.ds(at, 512)]
+        copy = pltpu.make_async_copy(stage, target, self.sem())
+        copy.start()
+        self.stores[slot] = copy
+
     def drain(self):
         for copy in self.sends + list(self.flying.values()):
             copy.wait_send()
@@ -607,14 +669,16 @@
 
     def attach(self, env, refs, sources, weights, results):
         self.b = refs
+        self.sources = sources
         self.held = weights
         self.results = results
         self.right_waits, self.left_waits, self.line_waits = {}, {}, {}
         self.loads = {}
-        for number, (source, weight) in enumerate(zip(sources, weights, strict=True)):
-            copy = pltpu.make_async_copy(source, weight, env.sem())
-            copy.start()
-            self.loads[number] = copy
+
+    def load(self, env, number):
+        copy = pltpu.make_async_copy(self.sources[number], self.held[number], env.sem())
+        copy.start()
+        self.loads[number] = copy
 
     def weight(self, number):
         if number in self.loads:
@@ -625,6 +689,7 @@
         r, t, n = self.rows, self.total, self.n
         vr, m = self.value_rows, self.message
         table = dict(
+            x=((r, 1024), BF),
             normed=((r, 1024), BF),
             s1=((n, m, 128), BF),
             r1=((n, m, 128), BF),
@@ -656,15 +721,25 @@
             acc=((r, 1024), F32),
             ps=((2, 4, r, 256), BF),
             pr=((2, 4, r, 256), BF),
-            fg=((4, r, 6144), BF),
-            ds=((4, r, 1024), BF),
-            dg=((4, r, 1024), BF),
-            sb=((4, 64, 6144), BF),
-            rb=((3, 64, 6144), BF),
-        )
-        if not self.packed:
+        )
+        if self.packed:
             table.update(
-                x=((r, 1024), BF),
+                ng=((4, 4, self.per, 1024), BF),
+                x7=((t, 256), BF),
+                s9=((n, m, 128), BF),
+                r9=((n, m, 128), BF),
+                fg=((4, r, 4608), BF),
+                ds=((4, r, 768), BF),
+                dg=((4, r, 768), BF),
+                sb=((4, 64, 4608), BF),
+                rb=((4, 64, 4608), BF),
+            )
+        else:
+            table.update(
+                fg=((4, 4, r, 1536), BF),
+                dg=((4, 4, r, 1024), BF),
+                sb=((4, 64, 1536), BF),
+                rb=((4, 64, 1536), BF),
                 same=((t, t), F32),
                 lab=((t, 128), BF),
                 hot=((2, self.per, 64), BF),
@@ -673,8 +748,7 @@
         return table
 
     def gain(self, env, which):
-        row = self.gains[which]
-        return env.b.vecs[row : row + 1, :]
+        return env.vector(self.gains[which])
 
     def pack(self, tile):
         if not self.packed:
@@ -697,11 +771,13 @@
             return [first]
         return [first, jnp.where(low, swap_halves(tile_a), tile_b)]
 
-    def project(self, env):
+    def project(self, env, then=None):
         hidden = self.b.x[...].astype(F32)
         normed = (hidden * inverse_rms(hidden) * self.gain(env, 0)).astype(BF)
         self.b.normed[...] = normed
         weight = self.weight(QKV)
+        if then is not None:
+            then()
         queries, keys, values = (dot(normed, weight[part]) for part in range(3))
         send = self.b.s1
         per = self.per
@@ -911,9 +987,12 @@
             rows = slice(i * per, (i + 1) * per)
             send[i, 0:per] = jnp.where(low, mixp[rows] * 0.125, swap_halves(dk[rows])).astype(BF)
             send[i, per:] = self.pack(dv[rows]).astype(BF)
+            if self.packed:
+                self.b.x7[rows, 0:128] = send[i, 0:per]
+                self.b.x7[rows, 128:256] = dv[rows].astype(BF)
         self.wait7 = env.exchange(send, self.b.r7)
 
-    def back_project(self, env, finish):
+    def back_project(self, env, finish, then=None):
         self.wait7()
         recv, dp = self.b.r7, self.b.dp
         per = self.per
@@ -930,6 +1009,8 @@
             dp[rows, 1024 + cols.start : 1024 + cols.stop] = tile.astype(BF)
 
         self.gather_heads(recv, per, put)
+        if then is not None:
+            then()
         weight = self.weight(QKV)
         acc = self.b.acc
 
@@ -956,26 +1037,23 @@
         right = (b.dp, b.mixl, b.gb, b.act)[which]
         return left, right
 
-    def share(self, env, which):
-        self.share_right(env, which)
-        self.share_left(env, which)
-
-    def share_right(self, env, which):
-        begin, size = COLS[which]
+    def share_right(self, env, which, begin=0, size=None):
+        at, full = COLS[which]
+        size = full if size is None else size
         _, right = self.parts(env, which)
         fg = self.b.fg
-        cols = pl.ds(begin, size)
-        fg[pl.ds(env.q, 1), :, begin : begin + size] = right[...][None]
+        cols = pl.ds(at + begin, size)
+        fg[pl.ds(env.q, 1), :, cols] = right[:, begin : begin + size][None]
         mine = fg.at[env.q, :, cols]
-        self.right_waits[which] = env.plane_send(
-            lambda other: mine, mine, fg.at[pl.ds(0, 3), :, cols]
+        self.right_waits.setdefault(which, []).append(
+            env.plane_send(lambda other: mine, mine, fg.at[pl.ds(0, 3), :, cols])
         )
 
     def share_left(self, env, which):
         left, _ = self.parts(env, which)
         ds, dg = self.b.ds, self.b.dg
         low = low_lanes(self.rows)
-        begin = 256 * which
+        begin = 256 * (which - 1)
         for a in range(2):
             tiles = [
                 left[:, 128 * (2 * z + a) : 128 * (2 * z + a) + 128].astype(F32) for z in range(4)
@@ -994,48 +1072,207 @@
         )
 
     def multiply(self, env, which):
-        self.right_waits[which]()
+        for wait in self.right_waits[which]:
+            wait()
         self.left_waits[which]()
         begin, size = COLS[which]
         fg, dg, sb, rb = self.b.fg, self.b.dg, self.b.sb, self.b.rb
         rows = 4 * self.rows
-        left = dg[:, :, 256 * which : 256 * which + 256].reshape(rows, 256)
+        left = dg[:, :, 256 * (which - 1) : 256 * which].reshape(rows, 256)
         for at in range(begin, begin + size, 512):
             right = fg[:, :, at : at + 512].reshape(rows, 512)
             product = dot_l(left, right)
             for z in range(4):
                 sb[z, :, at : at + 512] = product[64 * z : 64 * z + 64].astype(BF)
-        cols = pl.ds(begin, size)
-        self.line_waits[which] = env.line_send(
-            lambda other: sb.at[other, :, cols],
-            lambda step: rb.at[step - 1, :, cols],
-            rb.at[:, :, cols],
-        )
-
-    def collect(self, env, which):
-        self.line_waits[which]()
+        self.line_waits[which] = env.line_reduce(sb.at[:, :, pl.ds(begin, size)], rb.at[:, :, pl.ds(begin, size)])
+
+    def relay(self, env, which):
         begin, size = COLS[which]
         sb, rb = self.b.sb, self.b.rb
-        result = self.results[which]
+        arrived, pass_on, _ = self.line_waits[which]
+
+        @pl.when(env.middle)
+        def _():
+            arrived()
+            for at in range(begin, begin + size, 512):
+                cols = slice(at, at + 512)
+                far = pl.ds(env.far, 1)
+                total = sb[far, :, cols].astype(F32) + rb[3:4, :, cols].astype(F32)
+                sb[far, :, cols] = total.astype(BF)
+            pass_on()
+
+    def collect(self, env, which):
+        self.line_waits[which][2]()
+        begin, size = COLS[which]
+        sb, rb = self.b.sb, self.b.rb
         for at in range(0, size, 512):
             cols = slice(begin + at, begin + at + 512)
-            slot = env.stored % 4
-            env.stored += 1
-            if slot in env.stores:
-                env.stores.pop(slot).wait()
-            total = sb[pl.ds(env.z, 1), :, cols].astype(F32)
-            for step in range(1, 4):
-                total = total + rb[step - 1 : step, :, cols].astype(F32)
-            stage = env.b.stage
-            stage[slot] = total[0]
-            target = result.at[at // 512] if which == 0 else result.at[:, pl.ds(at, 512)]
-            copy = pltpu.make_async_copy(stage.at[slot], target, env.sem())
-            copy.start()
-            env.stores[slot] = copy
+
+            def fill(stage):
+                total = sb[pl.ds(env.z, 1), :, cols].astype(F32)
+                for slot in range(2):
+                    total = total + rb[slot : slot + 1, :, cols].astype(F32)
+                stage[...] = total[0]
+
+                @pl.when(env.middle)
+                def _():
+                    stage[...] += rb[2, :, cols].astype(F32)
+
+            env.store(self.results[which], which, at, fill)
+
+    def gather_line(self, env):
+        normed, ng, per = self.b.normed, self.b.ng, self.per
+        cols = pl.ds(pl.multiple_of(512 * env.c, 512), 512)
+
+        def rows(z):
+            return pl.ds(pl.multiple_of(lax.div(z, 2) * per, per), per)
+
+        ng[pl.ds(env.z, 1), pl.ds(env.q, 1), :, cols] = normed[rows(env.z), cols][None, None]
+        self.gather_wait = env.line_send(
+            lambda other: normed.at[rows(other), cols],
+            lambda step: ng.at[env.z, env.q, :, cols],
+            ng.at[pl.ds(0, 3), 0, :, cols],
+        )
+
+    def gather_plane(self, env):
+        self.gather_wait()
+        ng = self.b.ng
+        cols = pl.ds(pl.multiple_of(512 * env.c, 512), 512)
+        mine = ng.at[:, env.q, :, cols]
+        self.gather_wait = env.plane_send(lambda other: mine, mine, ng.at[:, pl.ds(0, 3), :, cols])
+
+    def gather_core(self, env):
+        self.gather_wait()
+        cols = pl.ds(pl.multiple_of(512 * env.c, 512), 512)
+        mine = self.b.ng.at[:, :, :, cols]
+        copy = env.remote(mine, mine, env.sem(), env.sem(), env.s, 1 - env.c)
+        copy.start()
+        env.sends.append(copy)
+        self.gather_wait = copy.wait_recv
+
+    def head_gradient(self, env):
+        self.gather_wait()
+        per, total = self.per, self.total
+        product = dot_l(self.b.x7[...], self.b.ng[...].reshape(total, 1024))
+        turned = jnp.transpose(product)
+        send = self.b.s9
+        for i in range(self.n):
+            rows = slice(i * 64, i * 64 + 64)
+            send[i, 0:per] = turned[rows, 0:128].astype(BF)
+            send[i, per:] = self.pack(turned[rows, 128:256]).astype(BF)
+        self.wait9 = env.exchange(send, self.b.r9)
+
+    def head_collect(self, env):
+        self.wait9()
+        recv, per, vr = self.b.r9, self.per, self.value_rows
+        low = low_lanes(per)
+
+        def both(pair, rows):
+            return recv[pair, rows].astype(F32) + recv[pair + 8, rows].astype(F32)
+
+        for part in range(3):
+
+            def fill(stage):
+                for j in range(4):
+                    cols = slice(128 * j, 128 * j + 128)
+                    rows = slice(0, per) if part < 2 else slice(per, per + vr)
+                    one, two = both(2 * j, rows), both(2 * j + 1, rows)
+                    if part == 0:
+                        stage[:, cols] = jnp.where(low, one, swap_halves(two))
+                    elif part == 1:
+                        stage[:, cols] = jnp.where(low, swap_halves(one), two)
+                    else:
+                        first, second = self.join_pairs(one, two)
+                        stage[0:vr, cols] = first
+                        stage[vr:, cols] = second
+
+            env.store(self.results[QKV], QKV, 512 * part, fill)
+
+    def spread_right(self, env, which):
+        _, right = self.parts(env, which)
+        fg, width = self.b.fg, WIDTHS[which]
+        cols = pl.ds(BEGINS[which], width)
+
+        def quarter(number):
+            return pl.ds(pl.multiple_of(number * width, 128), width)
+
+        fg[pl.ds(env.z, 1), pl.ds(env.q, 1), :, cols] = right[:, quarter(env.q)][None, None]
+        self.right_waits[which] = env.plane_send(
+            lambda other: right.at[:, quarter(other)],
+            fg.at[env.z, env.q, :, cols],
+            fg.at[env.z, pl.ds(0, 3), :, cols],
+        )
+
+    def spread_right_on(self, env, which):
+        self.right_waits[which]()
+        fg = self.b.fg
+        cols = pl.ds(BEGINS[which], WIDTHS[which])
+        mine = fg.at[env.z, :, :, cols]
+        self.right_waits[which] = env.line_send(
+            lambda other: mine, lambda step: mine, fg.at[pl.ds(0, 3), :, :, cols]
+        )
+
+    def spread_left(self, env, which):
+        left, _ = self.parts(env, which)
+        dg = self.b.dg
+        cols = pl.ds(256 * which, 256)
+
+        def quarter(number):
+            return pl.ds(pl.multiple_of(number * 256, 256), 256)
+
+        dg[pl.ds(env.z, 1), pl.ds(env.q, 1), :, cols] = left[:, quarter(env.z)][None, None]
+        self.left_waits[which] = env.line_send(
+            lambda other: left.at[:, quarter(other)],
+            lambda step: dg.at[env.z, env.q, :, cols],
+            dg.at[pl.ds(0, 3), env.q, :, cols],
+        )
+
+    def spread_left_on(self, env, which):
+        self.left_waits[which]()
+        dg = self.b.dg
+        cols = pl.ds(256 * which, 256)
+        mine = dg.at[:, env.q, :, cols]
+        self.left_waits[which] = env.plane_send(
+            lambda other: mine, mine, dg.at[:, pl.ds(0, 3), :, cols]
+        )
+
+    def spread_multiply(self, env, which):
+        self.right_waits[which]()
+        self.left_waits[which]()
+        fg, dg, sb, rb = self.b.fg, self.b.dg, self.b.sb, self.b.rb
+        width = WIDTHS[which]
+        cols = pl.ds(BEGINS[which], width)
+        rows = 16 * self.rows
+        product = dot_l(
+            dg[:, :, :, 256 * which : 256 * which + 256].reshape(rows, 256),
+            fg[:, :, :, cols].reshape(rows, width),
+        ).astype(BF)
+        for number in range(4):
+            sb[number, :, cols] = product[64 * number : 64 * number + 64]
+        rb[pl.ds(env.q, 1), :, cols] = sb[pl.ds(env.q, 1), :, cols]
+        self.line_waits[which] = env.plane_send(
+            lambda other: sb.at[other, :, cols],
+            rb.at[env.q, :, cols],
+            rb.at[pl.ds(0, 3), :, cols],
+        )
+
+    def spread_collect(self, env, which):
+        self.line_waits[which]()
+        rb, begin, width = self.b.rb, BEGINS[which], WIDTHS[which]
+        for at in range(0, SIZES[which], 512):
+
+            def fill(stage):
+                for inner in range(0, 512, 128):
+                    source, offset = divmod(at + inner, width)
+                    stage[:, inner : inner + 128] = rb[
+                        source, :, begin + offset : begin + offset + 128
+                    ].astype(F32)
+
+            env.store(self.results[which], which, at, fill)
 
 
 def pick_rows(env, dense, routed):
-    hot, labs, first = routed.b.hot, routed.b.labs, env.b.output
+    hot, labs, first = routed.b.hot, routed.b.labs, env.b.first
     group, slots = dense.per, routed.per
     base = env.s * group
     for seq in range(2):
@@ -1070,15 +1307,15 @@
 def gate_rows(env, dense, routed):
     group, slots = dense.per, routed.per
     sent = routed.b.acc[...].astype(BF)
-    router = env.b.vecs[4:5, :]
+    router = env.vector(4)
     grad_router = jnp.zeros((1, 1024), F32)
     for seq in range(2):
         rows = slice(seq * group, (seq + 1) * group)
-        first = env.b.output[rows, :]
+        first = env.b.first[rows, :]
         returned = restore(env, dense, routed, sent, seq)
         gate = jax.nn.sigmoid(jnp.sum(first * router, axis=1, keepdims=True))
         env.b.output[rows, :] = first + gate * returned
-        grad = env.b.cotangent[rows, :].astype(F32)
+        grad = env.b.cotangent[:, seq, :].astype(F32)
         low = (gate * grad).astype(BF)
         routed.b.e[seq * slots : (seq + 1) * slots, :] = dot(routed.b.hot[seq], low)
         logit = jnp.sum(grad * returned, axis=1, keepdims=True) * gate * (1.0 - gate)
@@ -1110,10 +1347,20 @@
 
 def whole_step(env, dense, routed):
     env.greet()
+    dense.load(env, QKV)
+    for seq in range(2):
+        dense.b.x[seq * dense.per : (seq + 1) * dense.per, :] = env.b.tokens[:, seq, :]
     env.b.vg[...] = jnp.zeros_like(env.b.vg)
+
     dense.project(env)
+    for number in (OUT, UP, DOWN):
+        dense.load(env, number)
+    dense.gather_line(env)
     dense.attend(env)
-    mid_d, first = dense.b.mid, env.b.output
+    for number in range(4):
+        routed.load(env, number)
+    dense.gather_plane(env)
+    mid_d, first = dense.b.mid, env.b.first
 
     def finish_dense(number, value):
         cols = slice(256 * number, 256 * number + 256)
@@ -1122,7 +1369,11 @@
     dense.feed(env, finish_dense)
     pick_rows(env, dense, routed)
     routed.project(env)
+    dense.gather_core(env)
+    dense.share_left(env, UP)
+    dense.share_right(env, OUT)
     routed.attend(env)
+    dense.share_right(env, DOWN, 0, 1024)
     mid_r, x_r, sent = routed.b.mid, routed.b.x, routed.b.acc
 
     def finish_routed(number, value):
@@ -1130,13 +1381,19 @@
         sent[:, cols] = mid_r[:, cols] - x_r[:, cols].astype(F32) + value
 
     routed.feed(env, finish_routed)
+    routed.spread_right(env, DOWN)
+    routed.spread_right(env, OUT)
+    routed.spread_left(env, QKV)
+    routed.spread_left(env, UP)
     gate_rows(env, dense, routed)
     routed.back_feed(env)
-    for which in (3, 2, 1):
-        routed.share(env, which)
+    routed.spread_right(env, UP)
+    routed.spread_left(env, DOWN)
+    routed.spread_left(env, OUT)
+    routed.spread_right_on(env, OUT)
     routed.back_attend(env)
-    for which in (3, 2, 1):
-        routed.multiply(env, which)
+    routed.spread_right_on(env, DOWN)
+    dense.share_right(env, DOWN, 1024, 1024)
 
     def finish_back(branch):
         low = branch.astype(BF)
@@ -1144,38 +1401,51 @@
             rows = slice(seq * dense.per, (seq + 1) * dense.per)
             dense.b.e[rows, :] += restore(env, dense, routed, low, seq)
 
-    routed.back_project(env, finish_back)
-    routed.share(env, 0)
+    routed.back_project(env, finish_back, lambda: routed.spread_right(env, QKV))
     dense.back_feed(env)
-    for which in (3, 2, 1):
-        dense.share(env, which)
-    routed.multiply(env, 0)
+    routed.spread_right_on(env, UP)
+    dense.share_left(env, DOWN)
+    dense.share_left(env, OUT)
+    dense.share_right(env, UP, 0, 1024)
+    routed.spread_left_on(env, DOWN)
+    routed.spread_left_on(env, OUT)
     dense.back_attend(env)
-    for which in (3, 2, 1):
-        dense.multiply(env, which)
+    dense.multiply(env, DOWN)
+    dense.head_gradient(env)
+    dense.multiply(env, OUT)
+    dense.share_right(env, UP, 1024, 1024)
+    routed.spread_right_on(env, QKV)
+    routed.spread_left_on(env, UP)
+    routed.spread_left_on(env, QKV)
 
     def finish_tokens(branch):
         env.b.grad_tokens[...] = dense.b.e[...] + branch
 
     dense.back_project(env, finish_tokens)
-    dense.share(env, 0)
     wait = share_vectors(env)
-    for which in (3, 2, 1, 0):
-        routed.collect(env, which)
-    dense.multiply(env, 0)
-    for which in (3, 2, 1, 0):
+    dense.multiply(env, UP)
+    dense.relay(env, DOWN)
+    dense.relay(env, OUT)
+    for which in (DOWN, OUT, UP, QKV):
+        routed.spread_multiply(env, which)
+    dense.relay(env, UP)
+    dense.head_collect(env)
+    for which in (DOWN, OUT, UP, QKV):
+        routed.spread_collect(env, which)
+    for which in (DOWN, OUT, UP):
         dense.collect(env, which)
     sum_vectors(env, wait)
     env.drain()
 
 
-def fused(group, tokens, cotangent, segments, routed_places, vecs, weights):
+def fused(group, tokens, cotangent, segments, routed_places, vectors, weights):
     n = lax.axis_size("seq")
     rows = 2 * group
     dense, routed = Layer(True, group, n), Layer(False, group // 4, n)
     wide = ((rows, 1024), F32)
     common = dict(
         stage=((4, 64, 512), F32),
+        first=wide,
         vg=((8, 1024), F32),
         sv=((n, 8, 128), F32),
         rv=((n, 8, 128), F32),
@@ -1191,23 +1461,20 @@
             del refs[:count]
             return taken
 
-        x, cotangent_ref, segments_ref, routed_ref, vecs_ref = take(5)
+        inputs = take(4)
+        vector_refs = take(5)
         sources = take(8)
-        output, grad_tokens, gvec = take(3)
+        outputs = take(3)
         results = take(8)
         held = take(8)
         dense_refs, routed_refs, common_refs = (
             types.SimpleNamespace(**dict(zip(table, take(len(table)), strict=True))) for table in groups
         )
-        dense_refs.x = x
-        common_refs.cotangent = cotangent_ref
-        common_refs.segments = segments_ref
-        common_refs.routed = routed_ref
-        common_refs.vecs = vecs_ref
-        common_refs.output = output
-        common_refs.grad_tokens = grad_tokens
-        common_refs.gvec = gvec
-        env = Env(common_refs, refs[0], n)
+        b = common_refs
+        b.tokens, b.cotangent, b.segments, b.routed = inputs
+        b.output, b.grad_tokens, b.gvec = outputs
+        b.vectors = vector_refs
+        env = Env(b, refs[0], n)
         dense.attach(env, dense_refs, sources[:4], held[:4], results[:4])
         routed.attach(env, routed_refs, sources[4:], held[4:], results[4:])
         whole_step(env, dense, routed)
@@ -1215,19 +1482,56 @@
     vmem = pl.BlockSpec(memory_space=pltpu.VMEM)
     hbm = pl.BlockSpec(memory_space=pl.ANY)
     outs = [wide, wide, ((8, 128), F32)] + [(shape, F32) for shape in GRADS * 2]
-    results = pl.pallas_call(
+    return pl.pallas_call(
         kernel,
         out_shape=[jax.ShapeDtypeStruct(*spec) for spec in outs],
-        in_specs=[vmem] * 5 + [hbm] * 8,
+        in_specs=[vmem] * 9 + [hbm] * 8,
         out_specs=[vmem] * 3 + [hbm] * 8,
         scratch_shapes=[pltpu.VMEM(shape, BF) for shape in SHAPES * 2]
         + [pltpu.VMEM(*spec) for spec in scratch]
-        + [pltpu.SemaphoreType.DMA((192,))],
+        + [pltpu.SemaphoreType.DMA((256,))],
         compiler_params=pltpu.CompilerParams(
             collective_id=0, has_side_effects=True, vmem_limit_bytes=LIMIT
         ),
-    )(tokens, cotangent, segments, routed_places, vecs, *weights)
-    return results[0], results[1], results[2], results[3:7], results[7:]
+    )(tokens, cotangent, segments, routed_places, *vectors, *weights)
+
+
+def place_results(group, parts):
+    def kernel(*refs):
+        output, grad_tokens, gvec = refs[:3]
+        grads, outs, held = refs[3:11], refs[11:26], refs[26:34]
+        sems = refs[34]
+        loads = [
+            pltpu.make_async_copy(source, target, sems.at[0, number])
+            for number, (source, target) in enumerate(zip(grads, held, strict=True))
+        ]
+        for copy in loads:
+            copy.start()
+        for source, target in ((output, outs[0]), (grad_tokens, outs[1])):
+            for seq in range(2):
+                target[:, seq, :] = source[seq * group : (seq + 1) * group, :]
+        for number in range(5):
+            outs[2 + number][...] = gvec[number, 0:64]
+        stores = []
+        for number, copy in enumerate(loads):
+            copy.wait()
+            stores.append(pltpu.make_async_copy(held[number], outs[7 + number], sems.at[1, number]))
+            stores[-1].start()
+        for copy in stores:
+            copy.wait()
+
+    vmem = pl.BlockSpec(memory_space=pltpu.VMEM)
+    hbm = pl.BlockSpec(memory_space=pl.ANY)
+    shapes = [(group, 2, 1024)] * 2 + [(64,)] * 5 + list(GRADS * 2)
+    return pl.pallas_call(
+        kernel,
+        out_shape=[jax.ShapeDtypeStruct(shape, F32) for shape in shapes],
+        in_specs=[vmem] * 3 + [hbm] * 8,
+        out_specs=[vmem] * 7 + [hbm] * 8,
+        scratch_shapes=[pltpu.VMEM(shape, F32) for shape in GRADS * 2]
+        + [pltpu.SemaphoreType.DMA((2, 8))],
+        compiler_params=pltpu.CompilerParams(vmem_limit_bytes=LIMIT),
+    )(*parts)
 
 
 def on_device_fused(
@@ -1249,22 +1553,14 @@
     routed_down,
     cotangent,
 ):
-    group, seqs, width = tokens.shape
-    zeros = jnp.zeros_like(router)
-    vecs = jnp.stack(
-        (dense_attn_gain, dense_mlp_gain, routed_attn_gain, routed_mlp_gain, router, zeros, zeros, zeros)
-    ).astype(F32)
-
-    def rows_of(array):
-        return jnp.transpose(array, (1, 0, 2)).reshape(seqs * group, width)
-
-    output, grad_tokens, gvec, dense_grads, routed_grads = fused(
+    group = tokens.shape[0]
+    parts = fused(
         group,
-        rows_of(tokens),
-        rows_of(cotangent),
+        tokens,
+        cotangent,
         segments,
         routed,
-        vecs,
+        (dense_attn_gain, dense_mlp_gain, routed_attn_gain, routed_mlp_gain, router),
         (
             jnp.transpose(dense_qkv, (1, 0, 2)),
             dense_out,
@@ -1276,28 +1572,24 @@
             routed_down,
         ),
     )
-
-    def back(array):
-        return jnp.transpose(array.reshape(seqs, group, width), (1, 0, 2))
-
-    def vector(row):
-        return gvec[row, 0:64]
+    placed = place_results(group, parts)
+    vectors = placed[2:7]
 
     def weights_of(grads, first, second):
         return (
-            vector(first),
+            vectors[first],
             jnp.transpose(grads[QKV], (1, 0, 2)),
             jnp.transpose(grads[OUT]),
-            vector(second),
+            vectors[second],
             grads[UP],
             jnp.transpose(grads[DOWN]),
         )
 
     return (
-        (back(output), back(grad_tokens))
-        + weights_of(dense_grads, 0, 1)
-        + weights_of(routed_grads, 2, 3)
-        + (vector(4),)
+        tuple(placed[:2])
+        + weights_of(placed[7:11], 0, 1)
+        + weights_of(placed[11:], 2, 3)
+        + (vectors[4],)
     )
 
 

time: 237 us -> 181 us (0.76)
  Pallas kernels: 213 us -> 177 us
  local copies, waits for them, and re-layouts: 20.4 us -> 0 us
    pallas_call x1, Pallas kernels: 213 us -> 172 us  [fused(): pl.pallas_call(kernel, out_shape=[jax.ShapeDtypeStruct(*spec) for spec in...]
    unnamed x18 -> x0, local copies, waits for them, and re-layouts: 9.01 us -> none
    transpose x3 -> x0, local copies, waits for them, and re-layouts: 6.52 us -> none  [the longest x2 3.41 us: rows_of(): return jnp.transpose(array, (1, 0, 2)).reshape(seqs * group, width)]
    pallas_call x0 -> x1, Pallas kernels: none -> 5.05 us  [place_results(): pl.pallas_call(kernel, out_shape=[jax.ShapeDtypeStruct(shape, F32) for sh...]
    another operation x8 -> x0, local copies, waits for them, and re-layouts: 3.49 us -> none  [on_device_fused(): jnp.stack((dense_attn_gain, dense_mlp_gain, routed_attn_gain, routed_mlp_...]
where the time goes in v2:
time: 181 us; the launch traced here: 178 us
  Pallas kernels  177 us (98%)
    pallas_call x1, Pallas kernels, fused(): pl.pallas_call(kernel, out_shape=[jax.ShapeDtypeStruct(*spec) for spec in...  172 us
    pallas_call x1, Pallas kernels, place_results(): pl.pallas_call(kernel, out_shape=[jax.ShapeDtypeStruct(shape, F32) for sh...  5.05 us

profile of v2, /device:TPU:0, one launch (start us, length us, event | category | flops | bytes accessed | tf_op | source)
XLA Modules:
  0.0 177.6 jit_solution(11588636918522416304)
XLA Ops:
  0.7 171.7 %shard_map.280 = (f32[128,1024]{1,0:T(8,128)}, f32[128,1024]{1,0:T(8,128)}, f32[8,128]{1,0:T(8,128)}, f32[3,64,512]{2,1,0:T(8,128)}, f32[64,512]{1,0:T(8,128)}, ...) custom-call(bf16[64,2,1024]{2,1,0:T(2,128)(2,1)} %refs_0_.1, ...), custom_call_target="tpu_custom_call" | custom-call | tf_op jit(solution)/shard_map/pallas_call | solution.py:1485
  172.4 5.0 %shard_map.281 = (f32[64,2,1024]{2,1,0:T(2,128)}, f32[64,2,1024]{2,1,0:T(2,128)}, f32[64]{0:T(128)}, f32[64]{0:T(128)}, f32[64]{0:T(128)}, /*index=5*/f32[64]{0:...) custom-call(f32[128,1024]{1,0:T(8,128)} %get-tuple-element.41.refs_0, ...), custom_call_target="tpu_custom_call" | custom-call | tf_op jit(solution)/shard_map/pallas_call | solution.py:1526

commit v3 on v2

--- a/solution.py
+++ b/solution.py
@@ -437,10 +437,11 @@
 LIMIT = 63 * 1024 * 1024
 F32 = jnp.float32
 MESH = pl.DeviceIdType.MESH
+PIECE = 1024
 WIDTHS = (384, 128, 512, 512)
 BEGINS = (0, 384, 512, 1024)
 SIZES = (1536, 512, 2048, 2048)
-COLS = (None, (0, 512), (512, 2048), (2560, 2048))
+COLS = (None, (0, 512), (512, 2048), None)
 
 
 def dot(a, b):
@@ -481,6 +482,7 @@
         self.sems = sems
         self.count = 0
         self.sends = []
+        self.middle_sends = []
         self.flying = {}
         self.stores = {}
         self.stored = 0
@@ -607,34 +609,68 @@
                 blocks.at[block], slots.at[slot], send[way], receive[slot], z * 4 + self.q, self.c
             )
 
-        copy(self.near, 0, 0, self.near).start()
-
-        @pl.when(self.middle)
-        def _():
-            copy(self.across, 1, 1, self.across).start()
-
         @pl.when(jnp.logical_not(self.middle))
         def _():
             copy(self.far, 3, 2, self.near).start()
-            copy(self.across, 2, 1, self.across).start()
+            copy(self.across, 2, 1, self.near).start()
+
+        copy(self.near, 0, 0, self.near).start()
 
         self.sends += [copy(0, 0, way, self.near) for way in range(3)]
 
-        def arrived():
-            copy(0, 3, 0, self.near).wait_recv()
-
-        def pass_on():
-            copy(self.far, 1, 2, self.far).start()
+        def arrived(slot):
+            copy(0, slot, 0, self.near).wait_recv()
+
+        def pass_on(slot):
+            block = (self.across, self.far)[slot - 2]
+            copy(block, 1, slot - 1, block).start()
 
         def finish():
-            copy(0, 0, 0, self.near).wait_recv()
-            copy(0, 1, 0, self.near).wait_recv()
-
+            for slot in range(2):
+                copy(0, slot, 0, self.near).wait_recv()
+
+        return arrived, pass_on, finish
+
+    def line_gather(self, ref):
+        self.meet()
+        receive = [self.sem() for _ in range(3)]
+        send = [self.sem() for _ in range(5)]
+
+        def copy(piece, way, slot, z):
+            return self.remote(
+                ref.at[piece], ref.at[piece], send[way], receive[slot], z * 4 + self.q, self.c
+            )
+
+        copy(self.z, 0, 0, self.near).start()
+
+        @pl.when(self.middle)
+        def _():
+            copy(self.z, 1, 1, self.across).start()
+
+        def second():
             @pl.when(self.middle)
             def _():
-                copy(0, 2, 0, self.near).wait_recv()
-
-        return arrived, pass_on, finish
+                copy(0, 0, 0, self.near).wait_recv()
+                copy(self.near, 2, 2, self.across).start()
+                copy(0, 0, 1, self.near).wait_recv()
+                copy(self.across, 3, 1, self.near).start()
+
+        def third():
+            @pl.when(self.middle)
+            def _():
+                copy(0, 0, 2, self.near).wait_recv()
+                copy(self.far, 4, 2, self.near).start()
+
+        self.sends.append(copy(0, 0, 0, self.near))
+        self.middle_sends += [copy(0, way, 0, self.near) for way in range(1, 5)]
+
+        def finish():
+            @pl.when(jnp.logical_not(self.middle))
+            def _():
+                for slot in range(3):
+                    copy(0, 0, slot, self.near).wait_recv()
+
+        return second, third, finish
 
     def store(self, result, which, at, fill):
         slot = self.stored % 4
@@ -654,6 +690,11 @@
         for copy in self.stores.values():
             copy.wait()
 
+        @pl.when(self.middle)
+        def _():
+            for copy in self.middle_sends:
+                copy.wait_send()
+
 
 class Layer:
     def __init__(self, packed, per, n):
@@ -672,7 +713,7 @@
         self.sources = sources
         self.held = weights
         self.results = results
-        self.right_waits, self.left_waits, self.line_waits = {}, {}, {}
+        self.right_waits, self.left_waits, self.line_waits, self.hops = {}, {}, {}, {}
         self.loads = {}
 
     def load(self, env, number):
@@ -728,11 +769,17 @@
                 x7=((t, 256), BF),
                 s9=((n, m, 128), BF),
                 r9=((n, m, 128), BF),
-                fg=((4, r, 4608), BF),
-                ds=((4, r, 768), BF),
-                dg=((4, r, 768), BF),
-                sb=((4, 64, 4608), BF),
-                rb=((4, 64, 4608), BF),
+                fg=((4, r, 2560), BF),
+                ds=((4, r, 512), BF),
+                dg=((4, r, 512), BF),
+                sb=((4, 64, 2560), BF),
+                rb=((4, 64, 2560), BF),
+                ul=((4, r, 1024), BF),
+                ur=((4, r, 512), BF),
+                us=((4, 256, 512), BF),
+                ub=((4, 256, 512), BF),
+                ux=((4, 64, 512), BF),
+                uy=((4, 64, 512), BF),
             )
         else:
             table.update(
@@ -867,7 +914,7 @@
                     begin = seq * per + number * vr
                     put(slice(begin, begin + vr), slice(128 * j, 128 * j + 128), tile)
 
-    def feed(self, env, finish):
+    def feed(self, env, finish, then=None):
         self.wait2()
         mixl = self.b.mixl
 
@@ -906,6 +953,8 @@
                 half
                 + 0.5 * before * (1.0 - bent * bent) * (0.7978845608028654 + 0.1070322243 * square)
             ).astype(BF)
+        if then is not None:
+            then()
         down = self.weight(DOWN)
         env.core_sum(
             self,
@@ -914,9 +963,11 @@
             finish,
         )
 
+    def round_incoming(self):
+        self.b.el[...] = self.b.e[...].astype(BF)
+
     def back_feed(self, env):
-        grad_low = self.b.e[...].astype(BF)
-        self.b.el[...] = grad_low
+        grad_low = self.b.el[...]
         down, up, out = self.weight(DOWN), self.weight(UP), self.weight(OUT)
         gb, slope = self.b.gb, self.b.gp
         for number in range(4):
@@ -1071,54 +1122,136 @@
             dg.at[pl.ds(0, 3), :, cols],
         )
 
-    def multiply(self, env, which):
-        for wait in self.right_waits[which]:
-            wait()
-        self.left_waits[which]()
+    def multiply(self, env, which, first=0, last=None):
+        if which in self.right_waits:
+            for wait in self.right_waits.pop(which):
+                wait()
+            self.left_waits[which]()
         begin, size = COLS[which]
+        last = size if last is None else last
         fg, dg, sb, rb = self.b.fg, self.b.dg, self.b.sb, self.b.rb
         rows = 4 * self.rows
         left = dg[:, :, 256 * (which - 1) : 256 * which].reshape(rows, 256)
-        for at in range(begin, begin + size, 512):
+        for at in range(begin + first, begin + last, 512):
             right = fg[:, :, at : at + 512].reshape(rows, 512)
             product = dot_l(left, right)
             for z in range(4):
                 sb[z, :, at : at + 512] = product[64 * z : 64 * z + 64].astype(BF)
-        self.line_waits[which] = env.line_reduce(sb.at[:, :, pl.ds(begin, size)], rb.at[:, :, pl.ds(begin, size)])
-
-    def relay(self, env, which):
-        begin, size = COLS[which]
+            if (at + 512 - begin) % PIECE == 0 or at + 512 == begin + last:
+                low = begin + (at - begin) // PIECE * PIECE
+                cols = pl.ds(low, at + 512 - low)
+                steps = env.line_reduce(sb.at[:, :, cols], rb.at[:, :, cols])
+                self.line_waits.setdefault(which, []).append((low, at + 512, steps))
+
+    def relay(self, env, which, pieces=None):
         sb, rb = self.b.sb, self.b.rb
-        arrived, pass_on, _ = self.line_waits[which]
-
-        @pl.when(env.middle)
-        def _():
-            arrived()
-            for at in range(begin, begin + size, 512):
+        for low, high, (arrived, pass_on, _) in self.line_waits[which][pieces or slice(None)]:
+
+            @pl.when(env.middle)
+            def _():
+                for slot, block in ((3, env.far), (2, env.across)):
+                    arrived(slot)
+                    for at in range(low, high, 512):
+                        cols = slice(at, at + 512)
+                        total = sb[pl.ds(block, 1), :, cols].astype(F32)
+                        total = total + rb[slot : slot + 1, :, cols].astype(F32)
+                        sb[pl.ds(block, 1), :, cols] = total.astype(BF)
+                    pass_on(slot)
+
+    def collect(self, env, which):
+        begin, _ = COLS[which]
+        sb, rb = self.b.sb, self.b.rb
+        for low, high, (_, _, finish) in self.line_waits[which]:
+            finish()
+            for at in range(low, high, 512):
                 cols = slice(at, at + 512)
-                far = pl.ds(env.far, 1)
-                total = sb[far, :, cols].astype(F32) + rb[3:4, :, cols].astype(F32)
-                sb[far, :, cols] = total.astype(BF)
-            pass_on()
-
-    def collect(self, env, which):
-        self.line_waits[which][2]()
-        begin, size = COLS[which]
-        sb, rb = self.b.sb, self.b.rb
-        for at in range(0, size, 512):
-            cols = slice(begin + at, begin + at + 512)
+
+                def fill(stage):
+                    total = sb[pl.ds(env.z, 1), :, cols].astype(F32)
+                    for slot in range(2):
+                        total = total + rb[slot : slot + 1, :, cols].astype(F32)
+                    stage[...] = total[0]
+
+                env.store(self.results[which], which, at - begin, fill)
+
+    def quarter_left(self, env):
+        ul, left = self.b.ul, self.b.el
+        cols = pl.ds(pl.multiple_of(512 * env.c, 512), 512)
+        ul[pl.ds(env.q, 1), :, cols] = left[:, cols][None]
+        self.quarter_wait = env.plane_send(
+            lambda other: left.at[:, cols], ul.at[env.q, :, cols], ul.at[pl.ds(0, 3), :, cols]
+        )
+
+    def quarter_core(self, env):
+        self.quarter_wait()
+        mine = self.b.ul.at[:, :, pl.ds(pl.multiple_of(512 * env.c, 512), 512)]
+        copy = env.remote(mine, mine, env.sem(), env.sem(), env.s, 1 - env.c)
+        copy.start()
+        env.sends.append(copy)
+        self.quarter_wait = copy.wait_recv
+
+    def quarter_right(self, env):
+        right, ur = self.b.act, self.b.ur
+
+        def quarter(number):
+            return pl.ds(pl.multiple_of(number * 512, 512), 512)
+
+        ur[pl.ds(env.q, 1)] = right[:, quarter(env.q)][None]
+        self.quarter_columns = env.plane_send(
+            lambda other: right.at[:, quarter(other)], ur.at[env.q], ur.at[pl.ds(0, 3)]
+        )
+
+    def quarter_multiply(self, env):
+        self.quarter_wait()
+        self.quarter_columns()
+        ul, ur, us, ub = self.b.ul, self.b.ur, self.b.us, self.b.ub
+        rows = 4 * self.rows
+        left = ul[...].reshape(rows, 1024)
+        self.quarter_steps = []
+        for at in range(0, 512, 256):
+            product = dot_l(left, ur[:, :, at : at + 256].reshape(rows, 256))
+            for z in range(4):
+                us[z, :, at : at + 256] = product[256 * z : 256 * z + 256].astype(BF)
+            cols = pl.ds(at, 256)
+            self.quarter_steps.append(env.line_reduce(us.at[:, :, cols], ub.at[:, :, cols]))
+
+    def quarter_relay(self, env):
+        us, ub = self.b.us, self.b.ub
+        for number, (arrived, pass_on, _) in enumerate(self.quarter_steps):
+            cols = slice(256 * number, 256 * number + 256)
+
+            @pl.when(env.middle)
+            def _():
+                for slot, block in ((3, env.far), (2, env.across)):
+                    arrived(slot)
+                    total = us[pl.ds(block, 1), :, cols].astype(F32)
+                    total = total + ub[slot : slot + 1, :, cols].astype(F32)
+                    us[pl.ds(block, 1), :, cols] = total.astype(BF)
+                    pass_on(slot)
+
+    def quarter_share(self, env):
+        us, ub, ux, uy = self.b.us, self.b.ub, self.b.ux, self.b.uy
+        for number, (_, _, finish) in enumerate(self.quarter_steps):
+            finish()
+            cols = slice(256 * number, 256 * number + 256)
+            total = us[pl.ds(env.z, 1), :, cols].astype(F32)
+            for slot in range(2):
+                total = total + ub[slot : slot + 1, :, cols].astype(F32)
+            for q in range(4):
+                ux[q, :, cols] = total[0, 64 * q : 64 * q + 64].astype(BF)
+        uy[pl.ds(env.q, 1)] = ux[pl.ds(env.q, 1)]
+        self.quarter_back = env.plane_send(
+            lambda other: ux.at[other], uy.at[env.q], uy.at[pl.ds(0, 3)]
+        )
+
+    def quarter_collect(self, env):
+        self.quarter_back()
+        for q in range(4):
 
             def fill(stage):
-                total = sb[pl.ds(env.z, 1), :, cols].astype(F32)
-                for slot in range(2):
-                    total = total + rb[slot : slot + 1, :, cols].astype(F32)
-                stage[...] = total[0]
-
-                @pl.when(env.middle)
-                def _():
-                    stage[...] += rb[2, :, cols].astype(F32)
-
-            env.store(self.results[which], which, at, fill)
+                stage[...] = self.b.uy[q].astype(F32)
+
+            env.store(self.results[DOWN], DOWN, 512 * q, fill)
 
     def gather_line(self, env):
         normed, ng, per = self.b.normed, self.b.ng, self.per
@@ -1207,10 +1340,10 @@
         self.right_waits[which]()
         fg = self.b.fg
         cols = pl.ds(BEGINS[which], WIDTHS[which])
-        mine = fg.at[env.z, :, :, cols]
-        self.right_waits[which] = env.line_send(
-            lambda other: mine, lambda step: mine, fg.at[pl.ds(0, 3), :, :, cols]
-        )
+        self.hops[which] = env.line_gather(fg.at[:, :, :, cols])
+
+    def spread_hop(self, env, which, number):
+        self.hops[which][number]()
 
     def spread_left(self, env, which):
         left, _ = self.parts(env, which)
@@ -1237,7 +1370,7 @@
         )
 
     def spread_multiply(self, env, which):
-        self.right_waits[which]()
+        self.hops[which][2]()
         self.left_waits[which]()
         fg, dg, sb, rb = self.b.fg, self.b.dg, self.b.sb, self.b.rb
         width = WIDTHS[which]
@@ -1373,27 +1506,32 @@
     dense.share_left(env, UP)
     dense.share_right(env, OUT)
     routed.attend(env)
-    dense.share_right(env, DOWN, 0, 1024)
     mid_r, x_r, sent = routed.b.mid, routed.b.x, routed.b.acc
 
     def finish_routed(number, value):
         cols = slice(256 * number, 256 * number + 256)
         sent[:, cols] = mid_r[:, cols] - x_r[:, cols].astype(F32) + value
 
-    routed.feed(env, finish_routed)
-    routed.spread_right(env, DOWN)
-    routed.spread_right(env, OUT)
+    def spread_early():
+        routed.spread_right(env, DOWN)
+        routed.spread_right(env, OUT)
+
+    routed.feed(env, finish_routed, spread_early)
+    dense.quarter_right(env)
     routed.spread_left(env, QKV)
     routed.spread_left(env, UP)
     gate_rows(env, dense, routed)
+    routed.round_incoming()
     routed.back_feed(env)
+    routed.spread_right_on(env, DOWN)
+    routed.spread_right_on(env, OUT)
     routed.spread_right(env, UP)
     routed.spread_left(env, DOWN)
     routed.spread_left(env, OUT)
-    routed.spread_right_on(env, OUT)
     routed.back_attend(env)
-    routed.spread_right_on(env, DOWN)
-    dense.share_right(env, DOWN, 1024, 1024)
+    routed.spread_hop(env, DOWN, 0)
+    routed.spread_hop(env, OUT, 0)
+    routed.spread_right_on(env, UP)
 
     def finish_back(branch):
         low = branch.astype(BF)
@@ -1402,19 +1540,25 @@
             dense.b.e[rows, :] += restore(env, dense, routed, low, seq)
 
     routed.back_project(env, finish_back, lambda: routed.spread_right(env, QKV))
+    dense.round_incoming()
+    dense.quarter_left(env)
     dense.back_feed(env)
-    routed.spread_right_on(env, UP)
-    dense.share_left(env, DOWN)
+    routed.spread_hop(env, DOWN, 1)
+    routed.spread_hop(env, OUT, 1)
+    routed.spread_hop(env, UP, 0)
+    routed.spread_right_on(env, QKV)
     dense.share_left(env, OUT)
     dense.share_right(env, UP, 0, 1024)
-    routed.spread_left_on(env, DOWN)
-    routed.spread_left_on(env, OUT)
+    dense.quarter_core(env)
     dense.back_attend(env)
-    dense.multiply(env, DOWN)
+    routed.spread_hop(env, UP, 1)
+    routed.spread_hop(env, QKV, 0)
+    dense.quarter_multiply(env)
     dense.head_gradient(env)
     dense.multiply(env, OUT)
     dense.share_right(env, UP, 1024, 1024)
-    routed.spread_right_on(env, QKV)
+    routed.spread_left_on(env, DOWN)
+    routed.spread_left_on(env, OUT)
     routed.spread_left_on(env, UP)
     routed.spread_left_on(env, QKV)
 
@@ -1422,19 +1566,23 @@
         env.b.grad_tokens[...] = dense.b.e[...] + branch
 
     dense.back_project(env, finish_tokens)
+    routed.spread_hop(env, QKV, 1)
     wait = share_vectors(env)
+    dense.quarter_relay(env)
+    dense.relay(env, OUT)
     dense.multiply(env, UP)
-    dense.relay(env, DOWN)
-    dense.relay(env, OUT)
-    for which in (DOWN, OUT, UP, QKV):
+    for which in (DOWN, OUT, UP):
         routed.spread_multiply(env, which)
     dense.relay(env, UP)
+    routed.spread_multiply(env, QKV)
+    dense.quarter_share(env)
     dense.head_collect(env)
     for which in (DOWN, OUT, UP, QKV):
         routed.spread_collect(env, which)
-    for which in (DOWN, OUT, UP):
+    for which in (OUT, UP):
         dense.collect(env, which)
     sum_vectors(env, wait)
+    dense.quarter_collect(env)
     env.drain()
 
 
@@ -1489,7 +1637,7 @@
         out_specs=[vmem] * 3 + [hbm] * 8,
         scratch_shapes=[pltpu.VMEM(shape, BF) for shape in SHAPES * 2]
         + [pltpu.VMEM(*spec) for spec in scratch]
-        + [pltpu.SemaphoreType.DMA((256,))],
+        + [pltpu.SemaphoreType.DMA((384,))],
         compiler_params=pltpu.CompilerParams(
             collective_id=0, has_side_effects=True, vmem_limit_bytes=LIMIT
         ),

time: 181 us -> 158 us (0.87); the launches traced: 178 us -> 157 us
  Pallas kernels: 177 us -> 156 us
    pallas_call x1, Pallas kernels: 172 us -> 151 us  [fused(): pl.pallas_call(kernel, out_shape=[jax.ShapeDtypeStruct(*spec) for spec in...]
where the time goes in v3:
time: 158 us; the launch traced here: 157 us
  Pallas kernels  156 us (99%)
    pallas_call x1, Pallas kernels, fused(): pl.pallas_call(kernel, out_shape=[jax.ShapeDtypeStruct(*spec) for spec in...  151 us
    pallas_call x1, Pallas kernels, place_results(): pl.pallas_call(kernel, out_shape=[jax.ShapeDtypeStruct(shape, F32) for sh...  5.05 us

profile of v3, /device:TPU:0, one launch (start us, length us, event | category | flops | bytes accessed | tf_op | source)
XLA Modules:
  0.0 157.1 jit_solution(1493013461205679699)
XLA Ops:
  0.7 151.3 %shard_map.280 = (f32[128,1024]{1,0:T(8,128)}, f32[128,1024]{1,0:T(8,128)}, f32[8,128]{1,0:T(8,128)}, f32[3,64,512]{2,1,0:T(8,128)}, f32[64,512]{1,0:T(8,128)}, ...) custom-call(bf16[64,2,1024]{2,1,0:T(2,128)(2,1)} %refs_0_.1, ...), custom_call_target="tpu_custom_call" | custom-call | tf_op jit(solution)/shard_map/pallas_call | solution.py:1633
  151.9 5.0 %shard_map.281 = (f32[64,2,1024]{2,1,0:T(2,128)}, f32[64,2,1024]{2,1,0:T(2,128)}, f32[64]{0:T(128)}, f32[64]{0:T(128)}, f32[64]{0:T(128)}, /*index=5*/f32[64]{0:...) custom-call(f32[128,1024]{1,0:T(8,128)} %get-tuple-element.41.refs_0, ...), custom_call_target="tpu_custom_call" | custom-call | tf_op jit(solution)/shard_map/pallas_call | solution.py:1674

commit v4 on v3

--- a/solution.py
+++ b/solution.py
@@ -1123,10 +1123,12 @@
         )
 
     def multiply(self, env, which, first=0, last=None):
-        if which in self.right_waits:
+        if first == 0:
+            self.left_waits[which]()
+        self.right_waits[which].pop(0)()
+        if last is None:
             for wait in self.right_waits.pop(which):
                 wait()
-            self.left_waits[which]()
         begin, size = COLS[which]
         last = size if last is None else last
         fg, dg, sb, rb = self.b.fg, self.b.dg, self.b.sb, self.b.rb
@@ -1348,11 +1350,11 @@
     def spread_left(self, env, which):
         left, _ = self.parts(env, which)
         dg = self.b.dg
-        cols = pl.ds(256 * which, 256)
 
         def quarter(number):
-            return pl.ds(pl.multiple_of(number * 256, 256), 256)
-
+            return pl.ds(pl.multiple_of(number * 256 + 128 * env.c, 128), 128)
+
+        cols = self.core_cols(env, which)
         dg[pl.ds(env.z, 1), pl.ds(env.q, 1), :, cols] = left[:, quarter(env.z)][None, None]
         self.left_waits[which] = env.line_send(
             lambda other: left.at[:, quarter(other)],
@@ -1360,14 +1362,25 @@
             dg.at[pl.ds(0, 3), env.q, :, cols],
         )
 
+    def core_cols(self, env, which):
+        return pl.ds(pl.multiple_of(256 * which + 128 * env.c, 128), 128)
+
     def spread_left_on(self, env, which):
         self.left_waits[which]()
         dg = self.b.dg
-        cols = pl.ds(256 * which, 256)
+        cols = self.core_cols(env, which)
         mine = dg.at[:, env.q, :, cols]
         self.left_waits[which] = env.plane_send(
             lambda other: mine, mine, dg.at[:, pl.ds(0, 3), :, cols]
         )
+
+    def spread_left_core(self, env, which):
+        self.left_waits[which]()
+        mine = self.b.dg.at[:, :, :, self.core_cols(env, which)]
+        copy = env.remote(mine, mine, env.sem(), env.sem(), env.s, 1 - env.c)
+        copy.start()
+        env.sends.append(copy)
+        self.left_waits[which] = copy.wait_recv
 
     def spread_multiply(self, env, which):
         self.hops[which][2]()
@@ -1480,49 +1493,53 @@
 
 def whole_step(env, dense, routed):
     env.greet()
+    b = env.b
+    copies = [
+        pltpu.make_async_copy(source, target, env.sem())
+        for source, target in ((b.tokens_hbm, b.tokens), (b.cotangent_hbm, b.cotangent))
+    ]
+    for copy in copies:
+        copy.start()
     dense.load(env, QKV)
+    copies[0].wait()
     for seq in range(2):
         dense.b.x[seq * dense.per : (seq + 1) * dense.per, :] = env.b.tokens[:, seq, :]
     env.b.vg[...] = jnp.zeros_like(env.b.vg)
-
     dense.project(env)
     for number in (OUT, UP, DOWN):
         dense.load(env, number)
+    dense.attend(env)
     dense.gather_line(env)
-    dense.attend(env)
     for number in range(4):
         routed.load(env, number)
-    dense.gather_plane(env)
     mid_d, first = dense.b.mid, env.b.first
-
     def finish_dense(number, value):
         cols = slice(256 * number, 256 * number + 256)
         first[:, cols] = mid_d[:, cols] + value
-
     dense.feed(env, finish_dense)
     pick_rows(env, dense, routed)
     routed.project(env)
-    dense.gather_core(env)
     dense.share_left(env, UP)
-    dense.share_right(env, OUT)
     routed.attend(env)
+    dense.gather_plane(env)
     mid_r, x_r, sent = routed.b.mid, routed.b.x, routed.b.acc
-
     def finish_routed(number, value):
         cols = slice(256 * number, 256 * number + 256)
         sent[:, cols] = mid_r[:, cols] - x_r[:, cols].astype(F32) + value
-
     def spread_early():
         routed.spread_right(env, DOWN)
         routed.spread_right(env, OUT)
-
     routed.feed(env, finish_routed, spread_early)
     dense.quarter_right(env)
     routed.spread_left(env, QKV)
     routed.spread_left(env, UP)
+    copies[1].wait()
     gate_rows(env, dense, routed)
+    out_copy = pltpu.make_async_copy(b.output, b.output_hbm, env.sem())
+    out_copy.start()
     routed.round_incoming()
     routed.back_feed(env)
+    dense.gather_core(env)
     routed.spread_right_on(env, DOWN)
     routed.spread_right_on(env, OUT)
     routed.spread_right(env, UP)
@@ -1531,14 +1548,13 @@
     routed.back_attend(env)
     routed.spread_hop(env, DOWN, 0)
     routed.spread_hop(env, OUT, 0)
+    dense.share_right(env, OUT)
     routed.spread_right_on(env, UP)
-
     def finish_back(branch):
         low = branch.astype(BF)
         for seq in range(2):
             rows = slice(seq * dense.per, (seq + 1) * dense.per)
             dense.b.e[rows, :] += restore(env, dense, routed, low, seq)
-
     routed.back_project(env, finish_back, lambda: routed.spread_right(env, QKV))
     dense.round_incoming()
     dense.quarter_left(env)
@@ -1549,40 +1565,50 @@
     routed.spread_right_on(env, QKV)
     dense.share_left(env, OUT)
     dense.share_right(env, UP, 0, 1024)
-    dense.quarter_core(env)
     dense.back_attend(env)
     routed.spread_hop(env, UP, 1)
     routed.spread_hop(env, QKV, 0)
+    dense.quarter_core(env)
     dense.quarter_multiply(env)
     dense.head_gradient(env)
     dense.multiply(env, OUT)
     dense.share_right(env, UP, 1024, 1024)
+    dense.multiply(env, UP, 0, 1024)
     routed.spread_left_on(env, DOWN)
     routed.spread_left_on(env, OUT)
     routed.spread_left_on(env, UP)
     routed.spread_left_on(env, QKV)
-
     def finish_tokens(branch):
         env.b.grad_tokens[...] = dense.b.e[...] + branch
-
     dense.back_project(env, finish_tokens)
+    grad_copy = pltpu.make_async_copy(b.grad_tokens, b.grad_tokens_hbm, env.sem())
+    grad_copy.start()
     routed.spread_hop(env, QKV, 1)
     wait = share_vectors(env)
     dense.quarter_relay(env)
     dense.relay(env, OUT)
-    dense.multiply(env, UP)
-    for which in (DOWN, OUT, UP):
-        routed.spread_multiply(env, which)
+    dense.multiply(env, UP, 1024, 2048)
+    routed.spread_left_core(env, DOWN)
+    routed.spread_left_core(env, OUT)
+    routed.spread_left_core(env, UP)
+    routed.spread_left_core(env, QKV)
+    routed.spread_multiply(env, DOWN)
+    routed.spread_multiply(env, QKV)
+    routed.spread_multiply(env, OUT)
+    routed.spread_multiply(env, UP)
     dense.relay(env, UP)
-    routed.spread_multiply(env, QKV)
     dense.quarter_share(env)
+    routed.spread_collect(env, DOWN)
     dense.head_collect(env)
-    for which in (DOWN, OUT, UP, QKV):
-        routed.spread_collect(env, which)
-    for which in (OUT, UP):
-        dense.collect(env, which)
+    routed.spread_collect(env, OUT)
+    routed.spread_collect(env, UP)
+    routed.spread_collect(env, QKV)
+    dense.collect(env, OUT)
+    dense.collect(env, UP)
     sum_vectors(env, wait)
     dense.quarter_collect(env)
+    out_copy.wait()
+    grad_copy.wait()
     env.drain()
 
 
@@ -1594,6 +1620,10 @@
     common = dict(
         stage=((4, 64, 512), F32),
         first=wide,
+        output=wide,
+        grad_tokens=wide,
+        tokens=((group, 2, 1024), BF),
+        cotangent=((group, 2, 1024), BF),
         vg=((8, 1024), F32),
         sv=((n, 8, 128), F32),
         rv=((n, 8, 128), F32),
@@ -1619,8 +1649,8 @@
             types.SimpleNamespace(**dict(zip(table, take(len(table)), strict=True))) for table in groups
         )
         b = common_refs
-        b.tokens, b.cotangent, b.segments, b.routed = inputs
-        b.output, b.grad_tokens, b.gvec = outputs
+        b.tokens_hbm, b.cotangent_hbm, b.segments, b.routed = inputs
+        b.output_hbm, b.grad_tokens_hbm, b.gvec = outputs
         b.vectors = vector_refs
         env = Env(b, refs[0], n)
         dense.attach(env, dense_refs, sources[:4], held[:4], results[:4])
@@ -1633,8 +1663,8 @@
     return pl.pallas_call(
         kernel,
         out_shape=[jax.ShapeDtypeStruct(*spec) for spec in outs],
-        in_specs=[vmem] * 9 + [hbm] * 8,
-        out_specs=[vmem] * 3 + [hbm] * 8,
+        in_specs=[hbm] * 2 + [vmem] * 7 + [hbm] * 8,
+        out_specs=[hbm] * 2 + [vmem] + [hbm] * 8,
         scratch_shapes=[pltpu.VMEM(shape, BF) for shape in SHAPES * 2]
         + [pltpu.VMEM(*spec) for spec in scratch]
         + [pltpu.SemaphoreType.DMA((384,))],
@@ -1646,38 +1676,47 @@
 
 def place_results(group, parts):
     def kernel(*refs):
-        output, grad_tokens, gvec = refs[:3]
-        grads, outs, held = refs[3:11], refs[11:26], refs[26:34]
-        sems = refs[34]
+        sources, outs, held, sems = refs[:11], refs[11:26], refs[26:38], refs[38]
+        gvec = sources[2]
+        grads = list(zip(sources[3:], held[:8], outs[7:], strict=True))
+        wides = list(zip(sources[:2], held[8:10], held[10:], outs[:2], strict=True))
         loads = [
-            pltpu.make_async_copy(source, target, sems.at[0, number])
-            for number, (source, target) in enumerate(zip(grads, held, strict=True))
+            pltpu.make_async_copy(item[0], item[1], sems.at[0, number])
+            for number, item in enumerate(wides + grads)
         ]
         for copy in loads:
             copy.start()
-        for source, target in ((output, outs[0]), (grad_tokens, outs[1])):
-            for seq in range(2):
-                target[:, seq, :] = source[seq * group : (seq + 1) * group, :]
         for number in range(5):
             outs[2 + number][...] = gvec[number, 0:64]
         stores = []
-        for number, copy in enumerate(loads):
-            copy.wait()
-            stores.append(pltpu.make_async_copy(held[number], outs[7 + number], sems.at[1, number]))
+
+        def store(source, target):
+            stores.append(pltpu.make_async_copy(source, target, sems.at[1, len(stores)]))
             stores[-1].start()
+
+        for number, (_, rows, turned, target) in enumerate(wides):
+            loads[number].wait()
+            for seq in range(2):
+                turned[:, seq, :] = rows[seq * group : (seq + 1) * group, :]
+            store(turned, target)
+        for number, (_, block, target) in enumerate(grads):
+            loads[2 + number].wait()
+            store(block, target)
         for copy in stores:
             copy.wait()
 
     vmem = pl.BlockSpec(memory_space=pltpu.VMEM)
     hbm = pl.BlockSpec(memory_space=pl.ANY)
-    shapes = [(group, 2, 1024)] * 2 + [(64,)] * 5 + list(GRADS * 2)
+    wide, turned = (2 * group, 1024), (group, 2, 1024)
+    shapes = [turned] * 2 + [(64,)] * 5 + list(GRADS * 2)
+    held = list(GRADS * 2) + [wide] * 2 + [turned] * 2
     return pl.pallas_call(
         kernel,
         out_shape=[jax.ShapeDtypeStruct(shape, F32) for shape in shapes],
-        in_specs=[vmem] * 3 + [hbm] * 8,
-        out_specs=[vmem] * 7 + [hbm] * 8,
-        scratch_shapes=[pltpu.VMEM(shape, F32) for shape in GRADS * 2]
-        + [pltpu.SemaphoreType.DMA((2, 8))],
+        in_specs=[hbm] * 2 + [vmem] + [hbm] * 8,
+        out_specs=[hbm] * 2 + [vmem] * 5 + [hbm] * 8,
+        scratch_shapes=[pltpu.VMEM(shape, F32) for shape in held]
+        + [pltpu.SemaphoreType.DMA((2, 10))],
         compiler_params=pltpu.CompilerParams(vmem_limit_bytes=LIMIT),
     )(*parts)
 

time: 158 us -> 151 us (0.956)
  Pallas kernels: 156 us -> 150 us
    pallas_call x1, Pallas kernels: 151 us -> 145 us  [fused(): pl.pallas_call(kernel, out_shape=[jax.ShapeDtypeStruct(*spec) for spec in...]
where the time goes in v4:
time: 151 us
  Pallas kernels  150 us (99%)
    pallas_call x1, Pallas kernels, fused(): pl.pallas_call(kernel, out_shape=[jax.ShapeDtypeStruct(*spec) for spec in...  145 us
    pallas_call x1, Pallas kernels, place_results(): pl.pallas_call(kernel, out_shape=[jax.ShapeDtypeStruct(shape, F32) for sh...  4.61 us

profile of v4, /device:TPU:0, one launch (start us, length us, event | category | flops | bytes accessed | tf_op | source)
XLA Modules:
  0.0 150.6 jit_solution(14856581793793746037)
XLA Ops:
  0.7 145.2 %shard_map.280 = (f32[128,1024]{1,0:T(8,128)}, f32[128,1024]{1,0:T(8,128)}, f32[8,128]{1,0:T(8,128)}, f32[3,64,512]{2,1,0:T(8,128)}, f32[64,512]{1,0:T(8,128)}, ...) custom-call(bf16[64,2,1024]{2,1,0:T(2,128)(2,1)} %refs_0_.1, ...), custom_call_target="tpu_custom_call" | custom-call | tf_op jit(solution)/shard_map/pallas_call | solution.py:1663
  145.8 4.6 %shard_map.281 = (f32[64,2,1024]{2,1,0:T(2,128)}, f32[64,2,1024]{2,1,0:T(2,128)}, f32[64]{0:T(128)}, f32[64]{0:T(128)}, f32[64]{0:T(128)}, /*index=5*/f32[64]{0:...) custom-call(f32[128,1024]{1,0:T(8,128)} %get-tuple-element.41.refs_0, ...), custom_call_target="tpu_custom_call" | custom-call | tf_op jit(solution)/shard_map/pallas_call | solution.py:1713

commit v5 on v4

--- a/solution.py
+++ b/solution.py
@@ -1519,7 +1519,6 @@
     dense.feed(env, finish_dense)
     pick_rows(env, dense, routed)
     routed.project(env)
-    dense.share_left(env, UP)
     routed.attend(env)
     dense.gather_plane(env)
     mid_r, x_r, sent = routed.b.mid, routed.b.x, routed.b.acc
@@ -1563,14 +1562,15 @@
     routed.spread_hop(env, OUT, 1)
     routed.spread_hop(env, UP, 0)
     routed.spread_right_on(env, QKV)
+    dense.share_left(env, UP)
     dense.share_left(env, OUT)
     dense.share_right(env, UP, 0, 1024)
     dense.back_attend(env)
-    routed.spread_hop(env, UP, 1)
-    routed.spread_hop(env, QKV, 0)
     dense.quarter_core(env)
     dense.quarter_multiply(env)
     dense.head_gradient(env)
+    routed.spread_hop(env, UP, 1)
+    routed.spread_hop(env, QKV, 0)
     dense.multiply(env, OUT)
     dense.share_right(env, UP, 1024, 1024)
     dense.multiply(env, UP, 0, 1024)

time: 151 us -> 151 us (level)
  no operation moved by 1% of the time
where the time goes in v5:
time: 151 us; the launch traced here: 150 us
  Pallas kernels  150 us (99%)
    pallas_call x1, Pallas kernels, fused(): pl.pallas_call(kernel, out_shape=[jax.ShapeDtypeStruct(*spec) for spec in...  145 us
    pallas_call x1, Pallas kernels, place_results(): pl.pallas_call(kernel, out_shape=[jax.ShapeDtypeStruct(shape, F32) for sh...  4.61 us

profile of v5, /device:TPU:0, one launch (start us, length us, event | category | flops | bytes accessed | tf_op | source)
XLA Modules:
  0.0 150.4 jit_solution(10209898911468857302)
XLA Ops:
  0.7 145.0 %shard_map.280 = (f32[128,1024]{1,0:T(8,128)}, f32[128,1024]{1,0:T(8,128)}, f32[8,128]{1,0:T(8,128)}, f32[3,64,512]{2,1,0:T(8,128)}, f32[64,512]{1,0:T(8,128)}, ...) custom-call(bf16[64,2,1024]{2,1,0:T(2,128)(2,1)} %refs_0_.1, ...), custom_call_target="tpu_custom_call" | custom-call | tf_op jit(solution)/shard_map/pallas_call | solution.py:1663
  145.6 4.6 %shard_map.281 = (f32[64,2,1024]{2,1,0:T(2,128)}, f32[64,2,1024]{2,1,0:T(2,128)}, f32[64]{0:T(128)}, f32[64]{0:T(128)}, f32[64]{0:T(128)}, /*index=5*/f32[64]{0:...) custom-call(f32[128,1024]{1,0:T(8,128)} %get-tuple-element.41.refs_0, ...), custom_call_target="tpu_custom_call" | custom-call | tf_op jit(solution)/shard_map/pallas_call | solution.py:1713

commit v6 on v4

--- a/solution.py
+++ b/solution.py
@@ -673,7 +673,7 @@
         return second, third, finish
 
     def store(self, result, which, at, fill):
-        slot = self.stored % 4
+        slot = self.stored % 8
         self.stored += 1
         if slot in self.stores:
             self.stores.pop(slot).wait()
@@ -1618,7 +1618,7 @@
     dense, routed = Layer(True, group, n), Layer(False, group // 4, n)
     wide = ((rows, 1024), F32)
     common = dict(
-        stage=((4, 64, 512), F32),
+        stage=((8, 64, 512), F32),
         first=wide,
         output=wide,
         grad_tokens=wide,

time: 151 us -> 150 us (level)
  no operation moved by 1% of the time
where the time goes in v6:
time: 150 us
  Pallas kernels  149 us (99%)
    pallas_call x1, Pallas kernels, fused(): pl.pallas_call(kernel, out_shape=[jax.ShapeDtypeStruct(*spec) for spec in...  145 us
    pallas_call x1, Pallas kernels, place_results(): pl.pallas_call(kernel, out_shape=[jax.ShapeDtypeStruct(shape, F32) for sh...  4.61 us

profile of v6, /device:TPU:0, one launch (start us, length us, event | category | flops | bytes accessed | tf_op | source)
XLA Modules:
  0.0 150.1 jit_solution(17515021756370207866)
XLA Ops:
  0.7 144.7 %shard_map.280 = (f32[128,1024]{1,0:T(8,128)}, f32[128,1024]{1,0:T(8,128)}, f32[8,128]{1,0:T(8,128)}, f32[3,64,512]{2,1,0:T(8,128)}, f32[64,512]{1,0:T(8,128)}, ...) custom-call(bf16[64,2,1024]{2,1,0:T(2,128)(2,1)} %refs_0_.1, ...), custom_call_target="tpu_custom_call" | custom-call | tf_op jit(solution)/shard_map/pallas_call | solution.py:1663
  145.3 4.6 %shard_map.281 = (f32[64,2,1024]{2,1,0:T(2,128)}, f32[64,2,1024]{2,1,0:T(2,128)}, f32[64]{0:T(128)}, f32[64]{0:T(128)}, f32[64]{0:T(128)}, /*index=5*/f32[64]{0:...) custom-call(f32[128,1024]{1,0:T(8,128)} %get-tuple-element.41.refs_0, ...), custom_call_target="tpu_custom_call" | custom-call | tf_op jit(solution)/shard_map/pallas_call | solution.py:1713
